TPU v7x, 256 devices: a whole 4x4x8 slice. The times are simulated.
256 devices in a mesh: blk: 32 (over z, y_lo, core), group: 8 (over y_hi, x).
Axes of the slice: x: 4, y: 4 (y_hi: 2, y_lo: 2; y = y_hi * 2 + y_lo), z: 8, core: 2. Of those that a mesh axis runs over, the one named last changes fastest.
Arguments:
- picture_embedding_matrix: float32 [32768, 1152], P(('blk', 'group')), may hold values from -4 to 4
- caption_embedding_matrix: float32 [32768, 1152], P(('blk', 'group')), may hold values from -4 to 4
- inverse_softness: float32 [1], replicated, may hold values from 8 to 12
- similarity_offset: float32 [1], replicated, may hold values from -4 to -2
Outputs:
- image_grad: float32 [32768, 1152], P(('blk', 'group'))
- text_gradient: float32 [32768, 1152], P(('blk', 'group'))
All inputs are finite; a program needn't handle non-finite values.
Results may differ from a plain program's by a relative error of at most 0.004.
Values may be sent and summed in bfloat16 or wider, within the bound.
A program may use at most 64 MiB of HBM per device.

v0:
```python
import jax
import jax.numpy as jnp
from jax import lax
from jax.sharding import PartitionSpec as P

EPS = 1e-06


def from_behind(block, axis, distance):
    devices = range(lax.axis_size(axis))
    route = [((i - distance) % len(devices), i) for i in devices]
    return lax.ppermute(block, axis, route)


def unit_rows(embed):
    inverse = lax.rsqrt(jnp.sum(embed * embed, axis=1, keepdims=True) + EPS)
    return (embed * inverse, inverse)


def per_device(
    picture_embedding_matrix, caption_embedding_matrix, inverse_softness, similarity_offset
):
    rows = picture_embedding_matrix.shape[0]
    width = picture_embedding_matrix.shape[1]
    blocks = lax.axis_size("blk")
    reach = blocks // 4 - 1
    here = lax.axis_index("blk")
    member = lax.axis_index("group")
    normed_picture_matrix, inv_image = unit_rows(picture_embedding_matrix)
    unit_text, inv_text = unit_rows(caption_embedding_matrix)
    image_bf = normed_picture_matrix.astype(jnp.bfloat16)
    caption_halfprecision = unit_text.astype(jnp.bfloat16)
    texts = lax.all_gather(caption_halfprecision, "group", axis=0, tiled=True)
    similarity_multiplier = inverse_softness[0]
    offset = similarity_offset[0]

    def owners_of(owner):
        return jnp.full((rows,), owner, jnp.int32)

    def score(images, owners, text_sum):
        logits = (
            jnp.einsum("rd,cd->rc", images, texts, preferred_element_type=jnp.float32)
            * similarity_multiplier
            + offset
        )
        within = lax.broadcasted_iota(jnp.int32, logits.shape, 0) % rows + member * rows
        column = lax.broadcasted_iota(jnp.int32, logits.shape, 1)
        target = jnp.where((owners[:, None] == here) & (column == within), 1.0, 0.0).astype(
            jnp.float32
        )
        coeff = (similarity_multiplier * (jax.nn.sigmoid(logits) - target)).astype(jnp.bfloat16)
        part_sum = jnp.dot(coeff, texts, preferred_element_type=jnp.float32)
        text_sum = text_sum + jnp.einsum(
            "rc,rd->cd", coeff, images, preferred_element_type=jnp.float32
        )
        return (part_sum, text_sum)

    text_zero = jnp.zeros((texts.shape[0], width), jnp.float32)
    images = from_behind(image_bf, "blk", -reach)
    carried, text_sum = score(images, owners_of((here + reach) % blocks), text_zero)

    def visit_carry(step, state):
        images, carried, text_sum = state
        images = from_behind(images, "blk", 1)
        carried = from_behind(carried, "blk", 1)
        owner = (here + reach - step) % blocks
        part_sum, text_sum = score(images, owners_of(owner), text_sum)
        return (images, carried + part_sum, text_sum)

    images, carried, text_sum = lax.fori_loop(
        1, 2 * reach + 1, visit_carry, (images, carried, text_sum)
    )
    image_dir = from_behind(carried, "blk", -reach)
    text_dir = lax.psum_scatter(text_sum, "group", scatter_dimension=0, tiled=True)
    image_grad = (
        image_dir
        - normed_picture_matrix * jnp.sum(normed_picture_matrix * image_dir, axis=1, keepdims=True)
    ) * inv_image
    text_gradient = (
        text_dir - unit_text * jnp.sum(unit_text * text_dir, axis=1, keepdims=True)
    ) * inv_text
    return (image_grad, text_gradient)


def solution(mesh):
    return jax.shard_map(
        per_device,
        mesh=mesh,
        in_specs=(P(("blk", "group"), None), P(("blk", "group"), None), P(), P()),
        out_specs=(P(("blk", "group"), None), P(("blk", "group"), None)),
        check_vma=False,
    )
```

profile of v0, /device:TPU:1, one launch (start us, length us, event | category | flops | bytes accessed | tf_op | source)
XLA Modules:
  0.0 409.9 jit_solution(8647620438423131875)
XLA Ops:
  11.7 8.5 %collective-permute-start.2 = (bf16[128,1152]{1,0:T(8,128)(2,1)S(1)}, bf16[128,1152]{1,0:T(8,128)(2,1)S(1)}, u32[]{:S(2)}, u32[]{:S(2)}) collective-permute-start(bf16[128,1152]{1,0:T(8,128)(2,1)S(1)} %multiply_convert_fusion.1), channel_id=1, source_target_pairs={{56,0},{64,8},{72,16},{80,24},{88,32},{96,40},{104,48},{112,56},{1... | collective-permute-start | bytes 884744 | tf_op jit(solution)/shard_map/ppermute | solution.py:12
  21.6 10.8 %collective-permute-done.2 = bf16[128,1152]{1,0:T(8,128)(2,1)S(1)} collective-permute-done((bf16[128,1152]{1,0:T(8,128)(2,1)S(1)}, bf16[128,1152]{1,0:T(8,128)(2,1)S(1)}, u32[]{:S(2)}, u32[]{:S(2)}) %collective-permute-start.2) | collective-permute-done | bytes 294944 | tf_op jit(solution)/shard_map/ppermute | solution.py:12
  32.4 43.7 %all-gather.2.cloned.1.call-done = bf16[1024,1152]{1,0:T(8,128)(2,1)} async-done(((bf16[128,1152]{1,0:T(8,128)(2,1)}), bf16[1024,1152]{1,0:T(8,128)(2,1)}) %all-gather.2.cloned.1.call-update) | async-done | bytes 2359312 | tf_op jit(solution)/shard_map/all_gather | solution.py:33
  76.1 2.8 fusion.16
  80.2 2.9 fusion.19
  83.2 216.4 %while.20 = (s32[]{:T(128)}, bf16[128,1152]{1,0:T(8,128)(2,1)S(1)}, f32[128,1152]{1,0:T(8,128)}, f32[1024,1152]{1,0:T(8,128)}, f32[]{:T(128)}, /*index=5*/bf16[1...) while((s32[]{:T(128)}, bf16[128,1152]{1,0:T(8,128)(2,1)S(1)}, ...), condition=%wide.region_3.4_spmd, body=%wide.region_2.3_spmd.sunk | while | flops 909001472 | bytes 58591900 | solution.py:70
  85.0 3.6 collective-permute-done
  99.0 3.5 collective-permute-done
  106.3 2.6 collective-permute-done.1
  113.7 4.4 %collective-permute-done = bf16[128,1152]{1,0:T(8,128)(2,1)S(1)} collective-permute-done((bf16[128,1152]{1,0:T(8,128)(2,1)S(1)}, bf16[128,1152]{1,0:T(8,128)(2,1)S(1)}, u32[]{:S(2)}, u32[]{:S(2)}) %collective-permute-start) | collective-permute-done | bytes 294944 | tf_op jit(solution)/shard_map/while/body/eval_jaxpr/ppermute | solution.py:12
  128.4 5.6 %collective-permute-done = bf16[128,1152]{1,0:T(8,128)(2,1)S(1)} collective-permute-done((bf16[128,1152]{1,0:T(8,128)(2,1)S(1)}, bf16[128,1152]{1,0:T(8,128)(2,1)S(1)}, u32[]{:S(2)}, u32[]{:S(2)}) %collective-permute-start) | collective-permute-done | bytes 294944 | tf_op jit(solution)/shard_map/while/body/eval_jaxpr/ppermute | solution.py:12
  140.3 2.8 collective-permute-start.1
  143.1 6.8 %collective-permute-done = bf16[128,1152]{1,0:T(8,128)(2,1)S(1)} collective-permute-done((bf16[128,1152]{1,0:T(8,128)(2,1)S(1)}, bf16[128,1152]{1,0:T(8,128)(2,1)S(1)}, u32[]{:S(2)}, u32[]{:S(2)}) %collective-permute-start) | collective-permute-done | bytes 294944 | tf_op jit(solution)/shard_map/while/body/eval_jaxpr/ppermute | solution.py:12
  157.9 8.1 %collective-permute-done = bf16[128,1152]{1,0:T(8,128)(2,1)S(1)} collective-permute-done((bf16[128,1152]{1,0:T(8,128)(2,1)S(1)}, bf16[128,1152]{1,0:T(8,128)(2,1)S(1)}, u32[]{:S(2)}, u32[]{:S(2)}) %collective-permute-start) | collective-permute-done | bytes 294944 | tf_op jit(solution)/shard_map/while/body/eval_jaxpr/ppermute | solution.py:12
  172.6 9.3 %collective-permute-done = bf16[128,1152]{1,0:T(8,128)(2,1)S(1)} collective-permute-done((bf16[128,1152]{1,0:T(8,128)(2,1)S(1)}, bf16[128,1152]{1,0:T(8,128)(2,1)S(1)}, u32[]{:S(2)}, u32[]{:S(2)}) %collective-permute-start) | collective-permute-done | bytes 294944 | tf_op jit(solution)/shard_map/while/body/eval_jaxpr/ppermute | solution.py:12
  188.0 9.8 %collective-permute-done = bf16[128,1152]{1,0:T(8,128)(2,1)S(1)} collective-permute-done((bf16[128,1152]{1,0:T(8,128)(2,1)S(1)}, bf16[128,1152]{1,0:T(8,128)(2,1)S(1)}, u32[]{:S(2)}, u32[]{:S(2)}) %collective-permute-start) | collective-permute-done | bytes 294944 | tf_op jit(solution)/shard_map/while/body/eval_jaxpr/ppermute | solution.py:12
  203.9 9.8 %collective-permute-done = bf16[128,1152]{1,0:T(8,128)(2,1)S(1)} collective-permute-done((bf16[128,1152]{1,0:T(8,128)(2,1)S(1)}, bf16[128,1152]{1,0:T(8,128)(2,1)S(1)}, u32[]{:S(2)}, u32[]{:S(2)}) %collective-permute-start) | collective-permute-done | bytes 294944 | tf_op jit(solution)/shard_map/while/body/eval_jaxpr/ppermute | solution.py:12
  219.9 9.8 %collective-permute-done = bf16[128,1152]{1,0:T(8,128)(2,1)S(1)} collective-permute-done((bf16[128,1152]{1,0:T(8,128)(2,1)S(1)}, bf16[128,1152]{1,0:T(8,128)(2,1)S(1)}, u32[]{:S(2)}, u32[]{:S(2)}) %collective-permute-start) | collective-permute-done | bytes 294944 | tf_op jit(solution)/shard_map/while/body/eval_jaxpr/ppermute | solution.py:12
  235.8 9.8 %collective-permute-done = bf16[128,1152]{1,0:T(8,128)(2,1)S(1)} collective-permute-done((bf16[128,1152]{1,0:T(8,128)(2,1)S(1)}, bf16[128,1152]{1,0:T(8,128)(2,1)S(1)}, u32[]{:S(2)}, u32[]{:S(2)}) %collective-permute-start) | collective-permute-done | bytes 294944 | tf_op jit(solution)/shard_map/while/body/eval_jaxpr/ppermute | solution.py:12
  251.7 9.8 %collective-permute-done = bf16[128,1152]{1,0:T(8,128)(2,1)S(1)} collective-permute-done((bf16[128,1152]{1,0:T(8,128)(2,1)S(1)}, bf16[128,1152]{1,0:T(8,128)(2,1)S(1)}, u32[]{:S(2)}, u32[]{:S(2)}) %collective-permute-start) | collective-permute-done | bytes 294944 | tf_op jit(solution)/shard_map/while/body/eval_jaxpr/ppermute | solution.py:12
  267.7 9.8 %collective-permute-done = bf16[128,1152]{1,0:T(8,128)(2,1)S(1)} collective-permute-done((bf16[128,1152]{1,0:T(8,128)(2,1)S(1)}, bf16[128,1152]{1,0:T(8,128)(2,1)S(1)}, u32[]{:S(2)}, u32[]{:S(2)}) %collective-permute-start) | collective-permute-done | bytes 294944 | tf_op jit(solution)/shard_map/while/body/eval_jaxpr/ppermute | solution.py:12
  283.6 9.8 %collective-permute-done = bf16[128,1152]{1,0:T(8,128)(2,1)S(1)} collective-permute-done((bf16[128,1152]{1,0:T(8,128)(2,1)S(1)}, bf16[128,1152]{1,0:T(8,128)(2,1)S(1)}, u32[]{:S(2)}, u32[]{:S(2)}) %collective-permute-start) | collective-permute-done | bytes 294944 | tf_op jit(solution)/shard_map/while/body/eval_jaxpr/ppermute | solution.py:12
  300.6 26.7 %collective-permute-done.3 = f32[128,1152]{1,0:T(8,128)S(1)} collective-permute-done((f32[128,1152]{1,0:T(8,128)S(1)}, f32[128,1152]{1,0:T(8,128)S(1)}, u32[]{:S(2)}, u32[]{:S(2)}) %collective-permute-start.3) | collective-permute-done | bytes 589856 | tf_op jit(solution)/shard_map/ppermute | solution.py:12
  328.5 71.2 %reduce-scatter.2.cloned.1.call-done = f32[128,1152]{1,0:T(8,128)} async-done(((f32[1024,1152]{1,0:T(8,128)}), f32[128,1152]{1,0:T(8,128)}) %reduce-scatter.2.cloned.1.call-update) | async-done | bytes 589840 | tf_op jit(solution)/shard_map/reduce_scatter | solution.py:74
  (208 shorter events, 111.7 us)
Async XLA Ops:
  7.2 68.9 %all-gather.2.cloned.1.call-start = ((), (), s32[]{:S(2)}) async-start(), calls=%async_computation.1 | async-start | bytes 2654208 | tf_op jit(solution)/shard_map/all_gather | solution.py:33
  10.4 389.3 %reduce-scatter.2.cloned.1.call-start = ((), (), s32[]{:S(2)}) async-start(), calls=%async_computation.2 | async-start | bytes 5308416 | tf_op jit(solution)/shard_map/reduce_scatter | solution.py:74
  11.7 20.6 %collective-permute-start.2 = (bf16[128,1152]{1,0:T(8,128)(2,1)S(1)}, bf16[128,1152]{1,0:T(8,128)(2,1)S(1)}, u32[]{:S(2)}, u32[]{:S(2)}) collective-permute-start(bf16[128,1152]{1,0:T(8,128)(2,1)S(1)} %multiply_convert_fusion.1), channel_id=1, source_target_pairs={{56,0},{64,8},{72,16},{80,24},{88,32},{96,40},{104,48},{112,56},{1... | collective-permute-start | bytes 884744 | tf_op jit(solution)/shard_map/ppermute | solution.py:12
  85.0 10.1 %collective-permute-start.1 = (f32[128,1152]{1,0:T(8,128)}, f32[128,1152]{1,0:T(8,128)S(1)}, u32[]{:S(2)}, u32[]{:S(2)}) collective-permute-start(f32[128,1152]{1,0:T(8,128)} %get-tuple-element.372), channel_id=1, source_target_pairs={{248,0},{0,8},{8,16},{16,24},{24,32},{32,40},{40,48},{48,56},{56,6... | collective-permute-start | bytes 1769480 | tf_op jit(solution)/shard_map/while/body/eval_jaxpr/ppermute | solution.py:12
  98.8 10.1 %collective-permute-start.1 = (f32[128,1152]{1,0:T(8,128)}, f32[128,1152]{1,0:T(8,128)S(1)}, u32[]{:S(2)}, u32[]{:S(2)}) collective-permute-start(f32[128,1152]{1,0:T(8,128)} %get-tuple-element.372), channel_id=1, source_target_pairs={{248,0},{0,8},{8,16},{16,24},{24,32},{32,40},{40,48},{48,56},{56,6... | collective-permute-start | bytes 1769480 | tf_op jit(solution)/shard_map/while/body/eval_jaxpr/ppermute | solution.py:12
  112.6 10.1 %collective-permute-start.1 = (f32[128,1152]{1,0:T(8,128)}, f32[128,1152]{1,0:T(8,128)S(1)}, u32[]{:S(2)}, u32[]{:S(2)}) collective-permute-start(f32[128,1152]{1,0:T(8,128)} %get-tuple-element.372), channel_id=1, source_target_pairs={{248,0},{0,8},{8,16},{16,24},{24,32},{32,40},{40,48},{48,56},{56,6... | collective-permute-start | bytes 1769480 | tf_op jit(solution)/shard_map/while/body/eval_jaxpr/ppermute | solution.py:12
  126.5 11.4 %collective-permute-start.1 = (f32[128,1152]{1,0:T(8,128)}, f32[128,1152]{1,0:T(8,128)S(1)}, u32[]{:S(2)}, u32[]{:S(2)}) collective-permute-start(f32[128,1152]{1,0:T(8,128)} %get-tuple-element.372), channel_id=1, source_target_pairs={{248,0},{0,8},{8,16},{16,24},{24,32},{32,40},{40,48},{48,56},{56,6... | collective-permute-start | bytes 1769480 | tf_op jit(solution)/shard_map/while/body/eval_jaxpr/ppermute | solution.py:12
  140.3 13.5 %collective-permute-start.1 = (f32[128,1152]{1,0:T(8,128)}, f32[128,1152]{1,0:T(8,128)S(1)}, u32[]{:S(2)}, u32[]{:S(2)}) collective-permute-start(f32[128,1152]{1,0:T(8,128)} %get-tuple-element.372), channel_id=1, source_target_pairs={{248,0},{0,8},{8,16},{16,24},{24,32},{32,40},{40,48},{48,56},{56,6... | collective-permute-start | bytes 1769480 | tf_op jit(solution)/shard_map/while/body/eval_jaxpr/ppermute | solution.py:12
  156.1 9.8 %collective-permute-start = (bf16[128,1152]{1,0:T(8,128)(2,1)S(1)}, bf16[128,1152]{1,0:T(8,128)(2,1)S(1)}, u32[]{:S(2)}, u32[]{:S(2)}) collective-permute-start(bf16[128,1152]{1,0:T(8,128)(2,1)S(1)} %get-tuple-element.371), channel_id=1, source_target_pairs={{248,0},{0,8},{8,16},{16,24},{24,32},{32,40},{40,48},{48,56},{56,6... | collective-permute-start | bytes 884744 | tf_op jit(solution)/shard_map/while/body/eval_jaxpr/ppermute | solution.py:12
  156.1 13.6 %collective-permute-start.1 = (f32[128,1152]{1,0:T(8,128)}, f32[128,1152]{1,0:T(8,128)S(1)}, u32[]{:S(2)}, u32[]{:S(2)}) collective-permute-start(f32[128,1152]{1,0:T(8,128)} %get-tuple-element.372), channel_id=1, source_target_pairs={{248,0},{0,8},{8,16},{16,24},{24,32},{32,40},{40,48},{48,56},{56,6... | collective-permute-start | bytes 1769480 | tf_op jit(solution)/shard_map/while/body/eval_jaxpr/ppermute | solution.py:12
  172.0 13.6 %collective-permute-start.1 = (f32[128,1152]{1,0:T(8,128)}, f32[128,1152]{1,0:T(8,128)S(1)}, u32[]{:S(2)}, u32[]{:S(2)}) collective-permute-start(f32[128,1152]{1,0:T(8,128)} %get-tuple-element.372), channel_id=1, source_target_pairs={{248,0},{0,8},{8,16},{16,24},{24,32},{32,40},{40,48},{48,56},{56,6... | collective-permute-start | bytes 1769480 | tf_op jit(solution)/shard_map/while/body/eval_jaxpr/ppermute | solution.py:12
  188.0 9.8 %collective-permute-start = (bf16[128,1152]{1,0:T(8,128)(2,1)S(1)}, bf16[128,1152]{1,0:T(8,128)(2,1)S(1)}, u32[]{:S(2)}, u32[]{:S(2)}) collective-permute-start(bf16[128,1152]{1,0:T(8,128)(2,1)S(1)} %get-tuple-element.371), channel_id=1, source_target_pairs={{248,0},{0,8},{8,16},{16,24},{24,32},{32,40},{40,48},{48,56},{56,6... | collective-permute-start | bytes 884744 | tf_op jit(solution)/shard_map/while/body/eval_jaxpr/ppermute | solution.py:12
  188.0 13.6 %collective-permute-start.1 = (f32[128,1152]{1,0:T(8,128)}, f32[128,1152]{1,0:T(8,128)S(1)}, u32[]{:S(2)}, u32[]{:S(2)}) collective-permute-start(f32[128,1152]{1,0:T(8,128)} %get-tuple-element.372), channel_id=1, source_target_pairs={{248,0},{0,8},{8,16},{16,24},{24,32},{32,40},{40,48},{48,56},{56,6... | collective-permute-start | bytes 1769480 | tf_op jit(solution)/shard_map/while/body/eval_jaxpr/ppermute | solution.py:12
  203.9 9.8 %collective-permute-start = (bf16[128,1152]{1,0:T(8,128)(2,1)S(1)}, bf16[128,1152]{1,0:T(8,128)(2,1)S(1)}, u32[]{:S(2)}, u32[]{:S(2)}) collective-permute-start(bf16[128,1152]{1,0:T(8,128)(2,1)S(1)} %get-tuple-element.371), channel_id=1, source_target_pairs={{248,0},{0,8},{8,16},{16,24},{24,32},{32,40},{40,48},{48,56},{56,6... | collective-permute-start | bytes 884744 | tf_op jit(solution)/shard_map/while/body/eval_jaxpr/ppermute | solution.py:12
  203.9 13.6 %collective-permute-start.1 = (f32[128,1152]{1,0:T(8,128)}, f32[128,1152]{1,0:T(8,128)S(1)}, u32[]{:S(2)}, u32[]{:S(2)}) collective-permute-start(f32[128,1152]{1,0:T(8,128)} %get-tuple-element.372), channel_id=1, source_target_pairs={{248,0},{0,8},{8,16},{16,24},{24,32},{32,40},{40,48},{48,56},{56,6... | collective-permute-start | bytes 1769480 | tf_op jit(solution)/shard_map/while/body/eval_jaxpr/ppermute | solution.py:12
  219.8 9.8 %collective-permute-start = (bf16[128,1152]{1,0:T(8,128)(2,1)S(1)}, bf16[128,1152]{1,0:T(8,128)(2,1)S(1)}, u32[]{:S(2)}, u32[]{:S(2)}) collective-permute-start(bf16[128,1152]{1,0:T(8,128)(2,1)S(1)} %get-tuple-element.371), channel_id=1, source_target_pairs={{248,0},{0,8},{8,16},{16,24},{24,32},{32,40},{40,48},{48,56},{56,6... | collective-permute-start | bytes 884744 | tf_op jit(solution)/shard_map/while/body/eval_jaxpr/ppermute | solution.py:12
  219.8 13.6 %collective-permute-start.1 = (f32[128,1152]{1,0:T(8,128)}, f32[128,1152]{1,0:T(8,128)S(1)}, u32[]{:S(2)}, u32[]{:S(2)}) collective-permute-start(f32[128,1152]{1,0:T(8,128)} %get-tuple-element.372), channel_id=1, source_target_pairs={{248,0},{0,8},{8,16},{16,24},{24,32},{32,40},{40,48},{48,56},{56,6... | collective-permute-start | bytes 1769480 | tf_op jit(solution)/shard_map/while/body/eval_jaxpr/ppermute | solution.py:12
  235.8 13.6 %collective-permute-start.1 = (f32[128,1152]{1,0:T(8,128)}, f32[128,1152]{1,0:T(8,128)S(1)}, u32[]{:S(2)}, u32[]{:S(2)}) collective-permute-start(f32[128,1152]{1,0:T(8,128)} %get-tuple-element.372), channel_id=1, source_target_pairs={{248,0},{0,8},{8,16},{16,24},{24,32},{32,40},{40,48},{48,56},{56,6... | collective-permute-start | bytes 1769480 | tf_op jit(solution)/shard_map/while/body/eval_jaxpr/ppermute | solution.py:12
  251.7 9.8 %collective-permute-start = (bf16[128,1152]{1,0:T(8,128)(2,1)S(1)}, bf16[128,1152]{1,0:T(8,128)(2,1)S(1)}, u32[]{:S(2)}, u32[]{:S(2)}) collective-permute-start(bf16[128,1152]{1,0:T(8,128)(2,1)S(1)} %get-tuple-element.371), channel_id=1, source_target_pairs={{248,0},{0,8},{8,16},{16,24},{24,32},{32,40},{40,48},{48,56},{56,6... | collective-permute-start | bytes 884744 | tf_op jit(solution)/shard_map/while/body/eval_jaxpr/ppermute | solution.py:12
  251.7 13.6 %collective-permute-start.1 = (f32[128,1152]{1,0:T(8,128)}, f32[128,1152]{1,0:T(8,128)S(1)}, u32[]{:S(2)}, u32[]{:S(2)}) collective-permute-start(f32[128,1152]{1,0:T(8,128)} %get-tuple-element.372), channel_id=1, source_target_pairs={{248,0},{0,8},{8,16},{16,24},{24,32},{32,40},{40,48},{48,56},{56,6... | collective-permute-start | bytes 1769480 | tf_op jit(solution)/shard_map/while/body/eval_jaxpr/ppermute | solution.py:12
  267.7 13.6 %collective-permute-start.1 = (f32[128,1152]{1,0:T(8,128)}, f32[128,1152]{1,0:T(8,128)S(1)}, u32[]{:S(2)}, u32[]{:S(2)}) collective-permute-start(f32[128,1152]{1,0:T(8,128)} %get-tuple-element.372), channel_id=1, source_target_pairs={{248,0},{0,8},{8,16},{16,24},{24,32},{32,40},{40,48},{48,56},{56,6... | collective-permute-start | bytes 1769480 | tf_op jit(solution)/shard_map/while/body/eval_jaxpr/ppermute | solution.py:12
  283.6 9.8 %collective-permute-start = (bf16[128,1152]{1,0:T(8,128)(2,1)S(1)}, bf16[128,1152]{1,0:T(8,128)(2,1)S(1)}, u32[]{:S(2)}, u32[]{:S(2)}) collective-permute-start(bf16[128,1152]{1,0:T(8,128)(2,1)S(1)} %get-tuple-element.371), channel_id=1, source_target_pairs={{248,0},{0,8},{8,16},{16,24},{24,32},{32,40},{40,48},{48,56},{56,6... | collective-permute-start | bytes 884744 | tf_op jit(solution)/shard_map/while/body/eval_jaxpr/ppermute | solution.py:12
  283.6 13.6 %collective-permute-start.1 = (f32[128,1152]{1,0:T(8,128)}, f32[128,1152]{1,0:T(8,128)S(1)}, u32[]{:S(2)}, u32[]{:S(2)}) collective-permute-start(f32[128,1152]{1,0:T(8,128)} %get-tuple-element.372), channel_id=1, source_target_pairs={{248,0},{0,8},{8,16},{16,24},{24,32},{32,40},{40,48},{48,56},{56,6... | collective-permute-start | bytes 1769480 | tf_op jit(solution)/shard_map/while/body/eval_jaxpr/ppermute | solution.py:12
  300.6 26.7 %collective-permute-start.3 = (f32[128,1152]{1,0:T(8,128)S(1)}, f32[128,1152]{1,0:T(8,128)S(1)}, u32[]{:S(2)}, u32[]{:S(2)}) collective-permute-start(f32[128,1152]{1,0:T(8,128)S(1)} %copy-done.6), channel_id=1, source_target_pairs={{56,0},{64,8},{72,16},{80,24},{88,32},{96,40},{104,48},{112,56},{1... | collective-permute-start | bytes 1769480 | tf_op jit(solution)/shard_map/ppermute | solution.py:12
  (41 other events, 276.8 us)
Sparse Core Ops, SparseCore 0:
  11.2 64.8 all-gather.1
  299.7 99.9 reduce-scatter.1
where the time goes:
time: 410 us
  waiting for transfers between devices  268 us (65%)
  matrix products  83 us (20%)
  starting transfers between devices  25.9 us (6%)
  between operations  15.4 us (4%)
  other arithmetic  9.05 us (2%)
  local copies, waits for them, and re-layouts  7.34 us (2%)
    ppermute x30, waiting for transfers between devices, from_behind(): return lax.ppermute(block, axis, route)  154 us
    reduce_scatter x1, waiting for transfers between devices, per_device(): lax.psum_scatter(text_sum, 'group', scatter_dimension=0, tiled=True)  71.2 us
    all_gather x1, waiting for transfers between devices, per_device(): texts = lax.all_gather(caption_halfprecision, 'group', axis=0, tiled=True)  43.7 us
    dot_general x15, matrix products, score(): jnp.einsum('rd,cd->rc', images, texts, preferred_element_type=jnp.float32)  38.5 us
    ppermute x30, starting transfers between devices, from_behind(): return lax.ppermute(block, axis, route)  25.8 us
    dot_general x15, matrix products, score(): part_sum = jnp.dot(coeff, texts, preferred_element_type=jnp.float32)  24.9 us
    dot_general x15, matrix products, score(): jnp.einsum('rc,rd->cd', coeff, images, preferred_element_type=jnp.float32)  19.6 us
  transfers between devices with their start and end apart: 32, of which 21 were waited for; matrix products, arithmetic and copies ran while one was open for 13% of the time, Pallas kernels for 0%

commit v1 on v0

v1 whole, which is shorter than its diff:
```python
import functools

import jax
import jax.numpy as jnp
from jax import lax
from jax.experimental import pallas as pl
from jax.experimental.pallas import tpu as pltpu
from jax.sharding import PartitionSpec as P

EPS = 1e-06
F32 = jnp.float32
BF16 = jnp.bfloat16

OWN, BEHIND, AHEAD, FAR = range(4)

IMG_Y, IMG_CORE, IMG_CORE_Y = 0, 1, 2
IMG_UP, IMG_DOWN, IMG_UP_Y, IMG_DOWN_Y = 3, 4, 5, 6
IMG_BEHIND_CORE, IMG_BEHIND_CORE_Y, IMG_AHEAD_CORE, IMG_AHEAD_CORE_Y = 7, 8, 9, 10
IMG_FAR_CORE, IMG_FAR_Y, IMG_FAR_CORE_Y = 11, 12, 13
TXT_Y = 14
TXT_RIGHT, TXT_LEFT, TXT_RIGHT2, TXT_LEFT2 = 15, 17, 19, 21
BACK = 23


def unit_rows(embed):
    inverse = lax.rsqrt(jnp.sum(embed * embed, axis=1, keepdims=True) + EPS)
    return embed * inverse, inverse


def kernel(
    scale_ref,
    offset_ref,
    image_ref,
    text_ref,
    image_grad_ref,
    text_grad_ref,
    imgs,
    txts,
    image_sum,
    text_sum,
    coeff_buf,
    coeff_t_buf,
    image_out,
    image_in,
    text_out,
    text_in,
    send_sem,
    recv_sem,
):
    rows, width = image_ref.shape
    half = rows // 2
    n_blk = lax.axis_size("blk")
    blk = lax.axis_index("blk")
    group = lax.axis_index("group")
    core = blk % 2
    y = (blk // 2) % 2

    def device(dz=0, flip=0, dx=0, flip_y=0):
        plane = (blk // 4 + dz + n_blk // 4) % (n_blk // 4)
        within = blk % 4
        if flip % 2:
            within = within + 1 - 2 * core
        if flip // 2:
            within = within + 2 - 4 * y
        x = (group % 4 + dx + 4) % 4
        upper = group // 4
        if flip_y:
            upper = 1 - upper
        return (plane * 4 + within, upper * 4 + x)

    mate = device(flip=1)
    y_near = device(flip=2)
    up, down = device(dz=1), device(dz=-1)
    cross = device(dz=2 * core - 1, flip=1)
    far_to = device(dz=1 - 2 * y)
    far_home = device(dz=2 * y - 1)
    right, left = device(dx=1), device(dx=-1)
    y_far = device(flip_y=1)
    cross_group = 2 - core
    far_group = 1 + y

    barrier = pltpu.get_barrier_semaphore()
    for partner in (mate, y_near, up, down, cross, right, left, y_far):
        pl.semaphore_signal(barrier, inc=1, device_id=partner, device_id_type=pl.DeviceIdType.MESH)

    def message(index, source, target, to):
        return pltpu.make_async_remote_copy(
            src_ref=source,
            dst_ref=target,
            send_sem=send_sem.at[index],
            recv_sem=recv_sem.at[index],
            device_id=to,
            device_id_type=pl.DeviceIdType.MESH,
        )

    def slot(k):
        return pl.ds(k * rows, rows)

    def img(g, k):
        return imgs.at[g, slot(k)]

    def txt(h, k):
        return txts.at[h, slot(k)]

    upper_part, lower_part = pl.ds(2 * rows, half), pl.ds(2 * rows + half, half)

    gather = {
        IMG_Y: (img(OWN, 0), img(OWN, 2), y_near),
        IMG_CORE: (img(OWN, 0), img(OWN, 1), mate),
        IMG_CORE_Y: (img(OWN, 2), img(OWN, 3), mate),
        IMG_UP: (img(OWN, 0), img(BEHIND, 0), up),
        IMG_DOWN: (img(OWN, 0), img(AHEAD, 0), down),
        IMG_UP_Y: (img(OWN, 2), img(BEHIND, 2), up),
        IMG_DOWN_Y: (img(OWN, 2), img(AHEAD, 2), down),
        IMG_BEHIND_CORE: (img(BEHIND, 0), img(BEHIND, 1), mate),
        IMG_BEHIND_CORE_Y: (img(BEHIND, 2), img(BEHIND, 3), mate),
        IMG_AHEAD_CORE: (img(AHEAD, 0), img(AHEAD, 1), mate),
        IMG_AHEAD_CORE_Y: (img(AHEAD, 2), img(AHEAD, 3), mate),
        IMG_FAR_CORE: (img(cross_group, 0), img(FAR, 1), cross),
        IMG_FAR_Y: (img(far_group, 2), img(FAR, 2), far_to),
        IMG_FAR_CORE_Y: (img(FAR, 2), img(FAR, 3), mate),
        TXT_Y: (txt(0, 0), txt(1, 0), y_far),
    }
    for h in range(2):
        gather[TXT_RIGHT + h] = (txt(h, 0), txt(h, 3), right)
        gather[TXT_LEFT + h] = (txt(h, 0), txt(h, 1), left)
        gather[TXT_RIGHT2 + h] = (
            txts.at[h, pl.ds(3 * rows, half)],
            txts.at[h, upper_part],
            right,
        )
        gather[TXT_LEFT2 + h] = (
            txts.at[h, pl.ds(rows + half, half)],
            txts.at[h, lower_part],
            left,
        )
    home = {
        IMG_FAR_Y: far_home,
        IMG_UP: down,
        IMG_DOWN: up,
        IMG_UP_Y: down,
        IMG_DOWN_Y: up,
    }
    for h in range(2):
        home[TXT_RIGHT + h] = home[TXT_RIGHT2 + h] = left
        home[TXT_LEFT + h] = home[TXT_LEFT2 + h] = right

    def back_buffers(index):
        if index < TXT_Y:
            return image_out.at[index], image_in.at[index]
        if index >= TXT_RIGHT2:
            return text_out.at[index - TXT_Y, pl.ds(0, half)], text_in.at[index - TXT_Y, pl.ds(0, half)]
        return text_out.at[index - TXT_Y], text_in.at[index - TXT_Y]

    def start(*indices):
        for index in indices:
            message(index, *gather[index]).start()

    def arrived(*indices):
        for index in indices:
            message(index, *gather[index]).wait_recv()

    def back_message(index):
        out, into = back_buffers(index)
        return message(BACK + index, out, into, home.get(index, gather[index][2]))

    def send_home(index, total, at):
        out, _ = back_buffers(index)
        out[...] = total[at].astype(BF16)
        back_message(index).start()

    def add_home(index, total, at):
        back_message(index).wait_recv()
        _, into = back_buffers(index)
        total[at] += into[...].astype(F32)

    scale = scale_ref[0]
    offset = offset_ref[0]
    unit_image, inv_image = unit_rows(image_ref[...])
    imgs[OWN, slot(0)] = unit_image.astype(BF16)
    unit_text, inv_text = unit_rows(text_ref[...])
    txts[0, slot(0)] = unit_text.astype(BF16)

    pl.semaphore_wait(barrier, 8)
    start(TXT_Y, IMG_Y, TXT_RIGHT, TXT_LEFT, IMG_UP, IMG_DOWN, IMG_CORE)
    image_sum[...] = jnp.zeros_like(image_sum)
    text_sum[...] = jnp.zeros_like(text_sum)
    imgs[FAR, slot(0)] = jnp.zeros((rows, width), BF16)
    arrived(IMG_Y)
    start(IMG_UP_Y, IMG_DOWN_Y, IMG_CORE_Y)
    arrived(TXT_Y)
    start(TXT_RIGHT + 1, TXT_LEFT + 1)
    arrived(IMG_UP, IMG_DOWN)
    start(IMG_FAR_CORE, IMG_BEHIND_CORE, IMG_AHEAD_CORE)
    arrived(TXT_RIGHT, TXT_LEFT)
    start(TXT_RIGHT2, TXT_LEFT2)
    arrived(IMG_UP_Y, IMG_DOWN_Y)
    start(IMG_FAR_Y, IMG_BEHIND_CORE_Y, IMG_AHEAD_CORE_Y)
    arrived(TXT_RIGHT + 1, TXT_LEFT + 1)
    start(TXT_RIGHT2 + 1, TXT_LEFT2 + 1)
    arrived(IMG_CORE, IMG_CORE_Y, TXT_RIGHT2, TXT_LEFT2)

    def coefficients(images, texts, target=None):
        logits = (
            lax.dot_general(images, texts, (((1,), (1,)), ((), ())), preferred_element_type=F32) * scale + offset
        )
        chance = 1.0 / (1.0 + jnp.exp(-logits))
        if target is not None:
            chance = chance - target
        return (scale * chance).astype(BF16)

    def tile(step, carry):
        h = step // 4
        turn = step % 4
        g = jnp.where(h == 0, turn, jnp.where(turn == 0, FAR, jnp.where(turn == 3, OWN, turn)))

        @pl.when(step == 1)
        def _():
            arrived(IMG_BEHIND_CORE, IMG_BEHIND_CORE_Y)

        @pl.when(step == 2)
        def _():
            arrived(IMG_AHEAD_CORE, IMG_AHEAD_CORE_Y)
            arrived(IMG_FAR_Y)
            start(IMG_FAR_CORE_Y)

        @pl.when(step == 3)
        def _():
            arrived(IMG_FAR_CORE, IMG_FAR_CORE_Y)

        @pl.when(step == 4)
        def _():
            arrived(TXT_RIGHT2 + 1, TXT_LEFT2 + 1)

        coeff = coefficients(imgs[g], txts[h])
        coeff_buf[...] = coeff
        coeff_t_buf[...] = coeff.T

        @pl.when(step == 0)
        def _():
            row = lax.broadcasted_iota(jnp.int32, (rows, rows), 0)
            column = lax.broadcasted_iota(jnp.int32, (rows, rows), 1)
            target = jnp.where(row == column, 1.0, 0.0).astype(F32)
            own = coefficients(imgs[OWN, slot(0)], txts[0, slot(0)], target)
            coeff_buf[:rows, :rows] = own
            coeff_t_buf[:rows, :rows] = own.T

        image_sum[g] += jnp.dot(coeff_buf[...], txts[h], preferred_element_type=F32)
        text_sum[h] += jnp.dot(coeff_t_buf[...], imgs[g], preferred_element_type=F32)
        return carry

    lax.fori_loop(0, 8, tile, 0)

    def text_part(h, k, begin=0, count=None):
        return (h, pl.ds(k * rows + begin, rows if count is None else count))

    for h in (1, 0):
        send_home(TXT_RIGHT2 + h, text_sum, text_part(h, 2, 0, half))
        send_home(TXT_LEFT2 + h, text_sum, text_part(h, 2, half, half))
    send_home(IMG_FAR_CORE_Y, image_sum, (FAR, slot(3)))
    send_home(IMG_FAR_CORE, image_sum, (FAR, slot(1)))
    send_home(IMG_BEHIND_CORE, image_sum, (BEHIND, slot(1)))
    send_home(IMG_BEHIND_CORE_Y, image_sum, (BEHIND, slot(3)))
    send_home(IMG_AHEAD_CORE, image_sum, (AHEAD, slot(1)))
    send_home(IMG_AHEAD_CORE_Y, image_sum, (AHEAD, slot(3)))
    send_home(IMG_CORE, image_sum, (OWN, slot(1)))
    send_home(IMG_CORE_Y, image_sum, (OWN, slot(3)))
    add_home(IMG_FAR_CORE_Y, image_sum, (FAR, slot(2)))
    send_home(IMG_FAR_Y, image_sum, (FAR, slot(2)))
    for h in (1, 0):
        add_home(TXT_RIGHT2 + h, text_sum, text_part(h, 3, 0, half))
        send_home(TXT_RIGHT + h, text_sum, text_part(h, 3))
        add_home(TXT_LEFT2 + h, text_sum, text_part(h, 1, half, half))
        send_home(TXT_LEFT + h, text_sum, text_part(h, 1))
    add_home(IMG_BEHIND_CORE, image_sum, (BEHIND, slot(0)))
    add_home(IMG_AHEAD_CORE, image_sum, (AHEAD, slot(0)))
    add_home(IMG_FAR_CORE, image_sum, (cross_group, slot(0)))
    send_home(IMG_UP, image_sum, (BEHIND, slot(0)))
    send_home(IMG_DOWN, image_sum, (AHEAD, slot(0)))
    add_home(IMG_BEHIND_CORE_Y, image_sum, (BEHIND, slot(2)))
    add_home(IMG_AHEAD_CORE_Y, image_sum, (AHEAD, slot(2)))
    add_home(IMG_FAR_Y, image_sum, (far_group, slot(2)))
    send_home(IMG_UP_Y, image_sum, (BEHIND, slot(2)))
    send_home(IMG_DOWN_Y, image_sum, (AHEAD, slot(2)))
    add_home(TXT_RIGHT + 1, text_sum, text_part(1, 0))
    add_home(TXT_LEFT + 1, text_sum, text_part(1, 0))
    send_home(TXT_Y, text_sum, text_part(1, 0))
    add_home(IMG_CORE_Y, image_sum, (OWN, slot(2)))
    add_home(IMG_UP_Y, image_sum, (OWN, slot(2)))
    add_home(IMG_DOWN_Y, image_sum, (OWN, slot(2)))
    send_home(IMG_Y, image_sum, (OWN, slot(2)))
    add_home(IMG_CORE, image_sum, (OWN, slot(0)))
    add_home(IMG_UP, image_sum, (OWN, slot(0)))
    add_home(IMG_DOWN, image_sum, (OWN, slot(0)))
    add_home(TXT_RIGHT, text_sum, text_part(0, 0))
    add_home(TXT_LEFT, text_sum, text_part(0, 0))
    add_home(TXT_Y, text_sum, text_part(0, 0))
    add_home(IMG_Y, image_sum, (OWN, slot(0)))

    def projected(embed, direction):
        unit, inverse = unit_rows(embed)
        return (direction - unit * jnp.sum(unit * direction, axis=1, keepdims=True)) * inverse

    image_grad_ref[...] = projected(image_ref[...], image_sum[OWN, slot(0)])
    text_grad_ref[...] = projected(text_ref[...], text_sum[0, slot(0)])

    for index in gather:
        message(index, *gather[index]).wait_send()
        back_message(index).wait_send()


def per_device(picture, caption, inverse_softness, similarity_offset):
    rows, width = picture.shape
    scalar = pl.BlockSpec(memory_space=pltpu.SMEM)
    whole = pl.BlockSpec(memory_space=pltpu.VMEM)
    pairs = 15 * rows * 8 * rows
    return pl.pallas_call(
        kernel,
        out_shape=(
            jax.ShapeDtypeStruct((rows, width), F32),
            jax.ShapeDtypeStruct((rows, width), F32),
        ),
        in_specs=[scalar, scalar, whole, whole],
        out_specs=(whole, whole),
        scratch_shapes=[
            pltpu.VMEM((4, 4 * rows, width), BF16),
            pltpu.VMEM((2, 4 * rows, width), BF16),
            pltpu.VMEM((4, 4 * rows, width), F32),
            pltpu.VMEM((2, 4 * rows, width), F32),
            pltpu.VMEM((4 * rows, 4 * rows), BF16),
            pltpu.VMEM((4 * rows, 4 * rows), BF16),
            pltpu.VMEM((14, rows, width), BF16),
            pltpu.VMEM((14, rows, width), BF16),
            pltpu.VMEM((9, rows, width), BF16),
            pltpu.VMEM((9, rows, width), BF16),
            pltpu.SemaphoreType.DMA((2 * BACK,)),
            pltpu.SemaphoreType.DMA((2 * BACK,)),
        ],
        compiler_params=pltpu.CompilerParams(
            collective_id=0, has_side_effects=True, vmem_limit_bytes=56 * 2**20
        ),
        cost_estimate=pl.CostEstimate(
            flops=6 * pairs * width, bytes_accessed=16 * rows * width, transcendentals=2 * pairs
        ),
    )(inverse_softness, similarity_offset, picture, caption)


def solution(mesh):
    spec = P(("blk", "group"), None)
    return jax.shard_map(
        per_device,
        mesh=mesh,
        in_specs=(spec, spec, P(), P()),
        out_specs=(spec, spec),
        check_vma=False,
    )
```

time: 410 us -> 95.9 us (0.23)
  waiting for transfers between devices: 268 us -> 0 us
  Pallas kernels: 0 us -> 91.1 us
  matrix products: 83 us -> 0 us
  starting transfers between devices: 25.9 us -> 0 us
  between operations: 15.4 us -> 1.94 us
  other arithmetic: 9.05 us -> 0 us
  local copies, waits for them, and re-layouts: 7.34 us -> 2.8 us
    ppermute x30 -> x0, waiting for transfers between devices: 154 us -> none  [from_behind(): return lax.ppermute(block, axis, route)]
    pallas_call x0 -> x1, Pallas kernels: none -> 91.1 us  [per_device(): pl.pallas_call(kernel, out_shape=(jax.ShapeDtypeStruct((rows, width), F32...]
    dot_general x45 -> x0, matrix products: 83 us -> none  [the longest x15 38.5 us: score(): jnp.einsum('rd,cd->rc', images, texts, preferred_element_type=jnp.float32)]
    reduce_scatter x1 -> x0, waiting for transfers between devices: 71.2 us -> none  [per_device(): lax.psum_scatter(text_sum, 'group', scatter_dimension=0, tiled=True)]
    all_gather x1 -> x0, waiting for transfers between devices: 43.7 us -> none  [per_device(): texts = lax.all_gather(caption_halfprecision, 'group', axis=0, tiled=True)]
    ppermute x30 -> x0, starting transfers between devices: 25.8 us -> none  [from_behind(): return lax.ppermute(block, axis, route)]
    while x70 -> x0, local copies, waits for them, and re-layouts: 6.3 us -> none
  transfers between devices with their start and end apart: 32 -> 0, of which waited for: 21 -> 0; matrix products, arithmetic and copies ran while one was open for 13% -> 0% of each run, Pallas kernels for 0% -> 0%
where the time goes in v1:
time: 95.9 us; the launch traced here: 95.8 us
  Pallas kernels  91.1 us (95%)
  local copies, waits for them, and re-layouts  2.8 us (3%)
  between operations  1.94 us (2%)
    pallas_call x1, Pallas kernels, per_device(): pl.pallas_call(kernel, out_shape=(jax.ShapeDtypeStruct((rows, width), F32...  91.1 us
    unnamed x4, local copies, waits for them, and re-layouts  2.8 us

profile of v1, /device:TPU:1, one launch (start us, length us, event | category | flops | bytes accessed | tf_op | source)
XLA Modules:
  0.0 95.8 jit_solution(6165532694041089558)
XLA Ops:
  1.9 91.1 %shard_map.59 = (f32[128,1152]{1,0:T(8,128)}, f32[128,1152]{1,0:T(8,128)}) custom-call(f32[1]{0:T(128)S(6)} %copy.8.scale_ref, f32[1]{0:T(128)S(6)} %copy.9.offset_ref, f32[128,1152]{1,0:T(8,128)} %image_ref.1, f32[128,1152]{1,0:T(8,128)} %text_ref.1), custom_call_target="tpu_custom_call" | custom-call | flops 13589544960 | bytes 2359296 | tf_op jit(solution)/shard_map/pallas_call | solution.py:317
  93.0 0.0 copy-start
  93.0 2.0 %copy.10 = f32[128,1152]{1,0:T(8,128)} copy(f32[128,1152]{1,0:T(8,128)} %get-tuple-element.4) | data formatting | bytes 1179648
  95.0 0.0 copy-done
  95.0 0.8 copy.11
Async XLA Ops:
  93.0 2.0 %copy-start = (f32[128,1152]{1,0:T(8,128)S(1)}, f32[128,1152]{1,0:T(8,128)}, u32[]{:S(2)}) copy-start(f32[128,1152]{1,0:T(8,128)} %get-tuple-element.5) | copy-start | bytes 1769476

commit v2 on v0

v2 whole, which is shorter than its diff:
```python
import functools

import jax
import jax.numpy as jnp
from jax import lax
from jax.experimental import pallas as pl
from jax.experimental.pallas import tpu as pltpu
from jax.sharding import PartitionSpec as P

EPS = 1e-06
F32 = jnp.float32
BF16 = jnp.bfloat16

OWN, FIRST, SECOND, FAR = range(4)
MESSAGES = 23

OPENING = (
    ("+TYa", "+TR0a", "+TL0b", "+IYa", "+GUa", "+HUa", "+TR0b", "+TL0a", "+TYb", "+IYb", "+GUb", "+HUb", "+IC"),
)
BEFORE = {
    0: (
        ("-IYa", "+GYa", "+HYa", "+JYa", "-TR0a", "+HR0a", "-TL0b", "+HL0b", "-GUa", "+F1a", "-HUa", "+MCa", "+PCa"),
        ("-IYb", "+GYb", "+HYb", "+JYb", "-TYa", "+TR1a", "+TL1a", "-GUb", "+F1b", "-HUb", "+MCb", "+PCb"),
        ("-TYb", "+TL1b", "+TR1b", "-GYa", "+F2a", "-HYa", "+KYa", "+LYa"),
        ("-IC", "-JY", "-TR0b", "-TL0a", "-HR0a", "-HL0b"),
    ),
    1: (("-TR1a", "+HR1a", "-TL1b", "+HL1b", "-MC", "-PC"),),
    2: (("-GYb", "+F2b", "-HYb", "+KYb", "+LYb", "-F2a", "+F3a", "-KY", "-LY"),),
    3: (("-F2b", "+F3b", "-F1", "-F3"),),
    4: (("<HR0a", "<HL0b", "<TR0b", "<TL0a", "-TR1b", "-TL1a", "-HR1a", "-HL1b"),),
    5: (("<F3a", "<F3b", "<F1a", "<F1b"),),
    6: (("<LYa", "<KYa", "<LYb", "<KYb", ">HR0a", "<TR0a", ">HL0b", "<TL0b"),),
    7: (("<PCa", "<MCa", "<PCb", "<MCb"),),
}
WITHIN = {
    5: ((">F3a", "<F2a", ">F3b", "<F2b"),),
    6: ((">LYa", "<HYa", ">LYb", "<HYb"),),
    7: ((">MCa", ">PCa", "<HUa", ">MCb", ">PCb", "<HUb", ">KY"),),
}
CLOSING = (
    ("<HR1a", "<HL1b", "<TR1b", "<TL1a", "<JY", "<IC", ">F2a", "<GYa", ">F2b", "<GYb", ">F1a", "<GUa", ">F1b", "<GUb"),
    (">HR1a", "<TR1a", ">HL1b", "<TL1b", ">JY", ">HY", ">TR0", ">TL0", ">IC", ">HU"),
    (">TR1b", ">TL1b", "<TYb", ">GYa", "<IYa", ">TR1a", ">TL1a", "<TYa", ">GYb", "<IYb", ">GU"),
    (">IYa", ">IYb"),
)
FINISH = ((">TYb", ">TYa"),)


def unit_rows(embed):
    inverse = lax.rsqrt(jnp.sum(embed * embed, axis=1, keepdims=True) + EPS)
    return embed * inverse, inverse


def kernel(
    scale_ref,
    offset_ref,
    image_ref,
    text_ref,
    image_grad_ref,
    text_grad_ref,
    imgs,
    txts,
    image_sum,
    text_sum,
    coeff_buf,
    coeff_t_buf,
    sums_out,
    sums_in,
    send_sem,
    recv_sem,
):
    rows, width = image_ref.shape
    half = rows // 2
    n_blk = lax.axis_size("blk")
    blk = lax.axis_index("blk")
    group = lax.axis_index("group")
    core = blk % 2
    y = (blk // 2) % 2

    def device(dz=0, flip=0, dx=0, flip_y=0):
        plane = (blk // 4 + dz + n_blk // 4) % (n_blk // 4)
        within = blk % 4
        if flip % 2:
            within = within + 1 - 2 * core
        if flip // 2:
            within = within + 2 - 4 * y
        x = (group % 4 + dx + 4) % 4
        upper = group // 4
        if flip_y:
            upper = 1 - upper
        return (plane * 4 + within, upper * 4 + x)

    mate, y_near, y_far = device(flip=1), device(flip=2), device(flip_y=1)
    right, left = device(dx=1), device(dx=-1)
    cross, cross_back = device(dz=2 * core - 1, flip=1), device(dz=1 - 2 * core)
    core_on = device(dz=2 * core - 1)
    y_on, y_back = device(dz=1 - 2 * y), device(dz=2 * y - 1)

    barrier = pltpu.get_barrier_semaphore()
    for partner in (mate, y_near, core_on, cross_back, cross, right, left, y_far):
        pl.semaphore_signal(barrier, inc=1, device_id=partner, device_id_type=pl.DeviceIdType.MESH)

    def img(g, k):
        return imgs, image_sum, g, k * rows

    def txt(h, k):
        return txts, text_sum, h, k * rows

    def pair(g, which, k):
        return imgs, image_sum, g, pl.multiple_of(which * 2 * rows, rows) + k * rows

    routes = {
        "IY": (img(OWN, 0), img(OWN, 2), y_near, y_near),
        "IC": (img(OWN, 0), img(OWN, 1), mate, mate),
        "JY": (img(OWN, 2), img(OWN, 3), mate, mate),
        "GU": (img(OWN, 0), pair(FIRST, 1 - core, 0), core_on, cross_back),
        "HU": (img(OWN, 0), pair(FIRST, core, 0), cross_back, core_on),
        "GY": (img(OWN, 2), pair(SECOND, y, 0), y_on, y_back),
        "HY": (img(OWN, 2), pair(SECOND, 1 - y, 0), y_back, y_on),
        "MC": (img(FIRST, 0), img(FIRST, 1), mate, mate),
        "PC": (img(FIRST, 2), img(FIRST, 3), mate, mate),
        "KY": (pair(SECOND, y, 0), pair(SECOND, y, 1), mate, mate),
        "LY": (pair(SECOND, 1 - y, 0), pair(SECOND, 1 - y, 1), mate, mate),
        "F1": (pair(FIRST, 1 - core, 0), img(FAR, 1), cross, cross),
        "F2": (pair(SECOND, y, 0), img(FAR, 2), y_on, y_back),
        "F3": (img(FAR, 2), img(FAR, 3), mate, mate),
        "TY": (txt(0, 0), txt(1, 0), y_far, y_far),
    }
    for h in range(2):
        routes[f"TR{h}"] = (txt(h, 0), txt(h, 3), right, left)
        routes[f"TL{h}"] = (txt(h, 0), txt(h, 1), left, right)
        routes[f"HR{h}"] = (txt(h, 3), txt(h, 2), right, left)
        routes[f"HL{h}"] = (txt(h, 1), txt(h, 2), left, right)
    names = list(routes)
    sent = []

    def copy(index, source, target, to):
        return pltpu.make_async_remote_copy(
            src_ref=source,
            dst_ref=target,
            send_sem=send_sem.at[index],
            recv_sem=recv_sem.at[index],
            device_id=to,
            device_id_type=pl.DeviceIdType.MESH,
        )

    def gather(name, part):
        (source, _, g, row), (target, _, g_to, row_to), to, _ = routes[name]
        return copy(
            2 * names.index(name) + part,
            source.at[g, pl.ds(row + part * half, half)],
            target.at[g_to, pl.ds(row_to + part * half, half)],
            to,
        )

    def back(name, part):
        index = 2 * names.index(name) + part
        return copy(2 * len(names) + index, sums_out.at[index], sums_in.at[index], routes[name][3])

    def act(event):
        parts = (0, 1)
        kind, name = event[0], event[1:]
        if name[-1] in "ab":
            parts, name = ("ab".index(name[-1]),), name[:-1]
        for part in parts:
            index = 2 * names.index(name) + part
            (_, into, g_into, row_into), (_, total, g, row), _, _ = routes[name]
            if kind == "+":
                gather(name, part).start()
                sent.append((gather, name, part))
            elif kind == "-":
                gather(name, part).wait_recv()
            elif kind == "<":
                sums_out[index] = total[g, pl.ds(row + part * half, half)].astype(BF16)
                back(name, part).start()
                sent.append((back, name, part))
            else:
                back(name, part).wait_recv()
                into[g_into, pl.ds(row_into + part * half, half)] += sums_in[index].astype(F32)

    def act_all(events):
        for line in events:
            for event in line:
                act(event)

    scale = scale_ref[0]
    offset = offset_ref[0]
    unit_image, inv_image = unit_rows(image_ref[...])
    imgs[OWN, :rows] = unit_image.astype(BF16)
    unit_text, inv_text = unit_rows(text_ref[...])
    txts[0, :rows] = unit_text.astype(BF16)

    pl.semaphore_wait(barrier, 8)
    act_all(OPENING)
    image_sum[...] = jnp.zeros_like(image_sum)
    text_sum[...] = jnp.zeros_like(text_sum)
    imgs[FAR, :rows] = jnp.zeros((rows, width), BF16)

    def coefficients(images, texts, target=None):
        logits = (
            lax.dot_general(images, texts, (((1,), (1,)), ((), ())), preferred_element_type=F32) * scale + offset
        )
        chance = 1.0 / (1.0 + jnp.exp(-logits))
        if target is not None:
            chance = chance - target
        return (scale * chance).astype(BF16)

    def tile(step, carry):
        h = step // 4
        g = jnp.where(h == 0, step, 7 - step)
        for when, events in BEFORE.items():
            pl.when(step == when)(functools.partial(act_all, events))

        coeff = coefficients(imgs[g], txts[h])
        coeff_buf[...] = coeff
        coeff_t_buf[...] = coeff.T

        @pl.when(step == 0)
        def _():
            row = lax.broadcasted_iota(jnp.int32, (rows, rows), 0)
            column = lax.broadcasted_iota(jnp.int32, (rows, rows), 1)
            target = jnp.where(row == column, 1.0, 0.0).astype(F32)
            own = coefficients(imgs[OWN, :rows], txts[0, :rows], target)
            coeff_buf[:rows, :rows] = own
            coeff_t_buf[:rows, :rows] = own.T

        for when, events in WITHIN.items():
            pl.when(step == when)(functools.partial(act_all, events))

        image_sum[g] += jnp.dot(coeff_buf[...], txts[h], preferred_element_type=F32)
        text_sum[h] += jnp.dot(coeff_t_buf[...], imgs[g], preferred_element_type=F32)
        return carry

    lax.fori_loop(0, 8, tile, 0)
    act_all(CLOSING)

    def projected(embed, direction):
        unit, inverse = unit_rows(embed)
        return (direction - unit * jnp.sum(unit * direction, axis=1, keepdims=True)) * inverse

    image_grad_ref[...] = projected(image_ref[...], image_sum[OWN, :rows])
    act_all(FINISH)
    text_grad_ref[...] = projected(text_ref[...], text_sum[0, :rows])

    for kind, name, part in sent:
        kind(name, part).wait_send()


def per_device(picture, caption, inverse_softness, similarity_offset):
    rows, width = picture.shape
    scalar = pl.BlockSpec(memory_space=pltpu.SMEM)
    whole = pl.BlockSpec(memory_space=pltpu.VMEM)
    pairs = 15 * rows * 8 * rows
    return pl.pallas_call(
        kernel,
        out_shape=(
            jax.ShapeDtypeStruct((rows, width), F32),
            jax.ShapeDtypeStruct((rows, width), F32),
        ),
        in_specs=[scalar, scalar, whole, whole],
        out_specs=(whole, whole),
        scratch_shapes=[
            pltpu.VMEM((4, 4 * rows, width), BF16),
            pltpu.VMEM((2, 4 * rows, width), BF16),
            pltpu.VMEM((4, 4 * rows, width), F32),
            pltpu.VMEM((2, 4 * rows, width), F32),
            pltpu.VMEM((4 * rows, 4 * rows), BF16),
            pltpu.VMEM((4 * rows, 4 * rows), BF16),
            pltpu.VMEM((2 * MESSAGES, rows // 2, width), BF16),
            pltpu.VMEM((2 * MESSAGES, rows // 2, width), BF16),
            pltpu.SemaphoreType.DMA((4 * MESSAGES,)),
            pltpu.SemaphoreType.DMA((4 * MESSAGES,)),
        ],
        compiler_params=pltpu.CompilerParams(
            collective_id=0, has_side_effects=True, vmem_limit_bytes=56 * 2**20
        ),
        cost_estimate=pl.CostEstimate(
            flops=6 * pairs * width, bytes_accessed=16 * rows * width, transcendentals=2 * pairs
        ),
    )(inverse_softness, similarity_offset, picture, caption)


def solution(mesh):
    spec = P(("blk", "group"), None)
    return jax.shard_map(
        per_device,
        mesh=mesh,
        in_specs=(spec, spec, P(), P()),
        out_specs=(spec, spec),
        check_vma=False,
    )
```

time: 410 us -> 89.2 us (0.22)
  waiting for transfers between devices: 268 us -> 0 us
  Pallas kernels: 0 us -> 83.4 us
  matrix products: 83 us -> 0 us
  starting transfers between devices: 25.9 us -> 0 us
  between operations: 15.4 us -> 1.94 us
  other arithmetic: 9.05 us -> 0 us
  local copies, waits for them, and re-layouts: 7.34 us -> 2.8 us
    ppermute x30 -> x0, waiting for transfers between devices: 154 us -> none  [from_behind(): return lax.ppermute(block, axis, route)]
    pallas_call x0 -> x1, Pallas kernels: none -> 83.4 us  [per_device(): pl.pallas_call(kernel, out_shape=(jax.ShapeDtypeStruct((rows, width), F32...]
    dot_general x45 -> x0, matrix products: 83 us -> none  [the longest x15 38.5 us: score(): jnp.einsum('rd,cd->rc', images, texts, preferred_element_type=jnp.float32)]
    reduce_scatter x1 -> x0, waiting for transfers between devices: 71.2 us -> none  [per_device(): lax.psum_scatter(text_sum, 'group', scatter_dimension=0, tiled=True)]
    all_gather x1 -> x0, waiting for transfers between devices: 43.7 us -> none  [per_device(): texts = lax.all_gather(caption_halfprecision, 'group', axis=0, tiled=True)]
    ppermute x30 -> x0, starting transfers between devices: 25.8 us -> none  [from_behind(): return lax.ppermute(block, axis, route)]
    while x70 -> x0, local copies, waits for them, and re-layouts: 6.3 us -> none
  transfers between devices with their start and end apart: 32 -> 0, of which waited for: 21 -> 0; matrix products, arithmetic and copies ran while one was open for 13% -> 0% of each run, Pallas kernels for 0% -> 0%
where the time goes in v2:
time: 89.2 us; the launch traced here: 88.1 us
  Pallas kernels  83.4 us (93%)
  local copies, waits for them, and re-layouts  2.8 us (3%)
  between operations  1.94 us (2%)
    pallas_call x1, Pallas kernels, per_device(): pl.pallas_call(kernel, out_shape=(jax.ShapeDtypeStruct((rows, width), F32...  83.4 us
    unnamed x4, local copies, waits for them, and re-layouts  2.8 us

profile of v2, /device:TPU:1, one launch (start us, length us, event | category | flops | bytes accessed | tf_op | source)
XLA Modules:
  0.0 88.1 jit_solution(11990303495293405232)
XLA Ops:
  1.9 83.4 %shard_map.59 = (f32[128,1152]{1,0:T(8,128)}, f32[128,1152]{1,0:T(8,128)}) custom-call(f32[1]{0:T(128)S(6)} %copy.8.scale_ref, f32[1]{0:T(128)S(6)} %copy.9.offset_ref, f32[128,1152]{1,0:T(8,128)} %image_ref.1, f32[128,1152]{1,0:T(8,128)} %text_ref.1), custom_call_target="tpu_custom_call" | custom-call | flops 13589544960 | bytes 2359296 | tf_op jit(solution)/shard_map/pallas_call | solution.py:254
  85.3 0.0 copy-start
  85.3 2.0 %copy.10 = f32[128,1152]{1,0:T(8,128)} copy(f32[128,1152]{1,0:T(8,128)} %get-tuple-element.4) | data formatting | bytes 1179648
  87.3 0.0 copy-done
  87.3 0.8 copy.11
Async XLA Ops:
  85.3 2.0 %copy-start = (f32[128,1152]{1,0:T(8,128)S(1)}, f32[128,1152]{1,0:T(8,128)}, u32[]{:S(2)}) copy-start(f32[128,1152]{1,0:T(8,128)} %get-tuple-element.5) | copy-start | bytes 1769476

commit v3 on v2

v3 whole, which is shorter than its diff:
```python
import functools

import jax
import jax.numpy as jnp
from jax import lax
from jax.experimental import pallas as pl
from jax.experimental.pallas import tpu as pltpu
from jax.sharding import PartitionSpec as P

EPS = 1e-06
LOG2_E = 1.4426950408889634
F32 = jnp.float32
BF16 = jnp.bfloat16

UNITS = 8
MESSAGES = 24

OPENING = (
    ("+IYa", "+TYa", "+AUa", "+BUa", "+TR0a", "+TL0b", "+TYb", "+AUb", "+BUb", "+TR0b", "+TL0a", "+IC"),
)
ORDER = (
    (0, 0), (2, 0), (3, 0), (6, 0), (1, 0), (8, 0), (7, 0), (9, 0),
    (7, 1), (6, 1), (8, 1), (9, 1), (2, 1), (3, 1), (1, 1), (0, 1),
)
BEFORE = {
    0: (
        ("-IYa", "+GYa", "+ZYa", "+JYa", "-AUa", "-BUa", "+MCa", "+PCa", "-TR0a", "+HR0a", "-TL0b", "+HL0b"),
        ("-TYa", "+TR1a", "+TL1a", "-AUb", "-BUb", "+SYb", "+IYb", "+F1", "+MCb", "+PCb"),
        ("-TYb", "+TR1b", "+TL1b", "-IC", "-TR0b", "-TL0a", "-HR0a", "-HL0b"),
    ),
    1: (("-GYa", "+F2a", "+KYa", "-MC", "-PC"),),
    2: (("-TR1a", "+HR1a", "-TL1b", "+HL1b"),),
    3: (("-SYb", "+F2b", "+KYb", "-F1"),),
    4: (("-IYb", "+ZYb", "+JYb", "-JY"),),
    5: (("-ZYa", "+LYa", "-KY"),),
    6: (("-F2a", "+F3a", "-F2b", "+F3b", "-F3"),),
    7: (("-ZYb", "+LYb", "-LY"),),
    8: (("<HR0a", "<HL0b", "<TR0b", "<TL0a", "-TR1b", "-TL1a", "-HR1a", "-HL1b"),),
    9: (("<F3",),),
    10: ((">F3a", "<F2a", ">F3b", "<F2b", "<F1"),),
    11: (("<KY",),),
    12: (("<LY", ">KY", ">HR0a", "<TR0a", ">HL0b", "<TL0b"),),
    13: ((">LY", "<ZY"),),
    14: (("<MC", "<PC", ">F2a", "<GYa"),),
    15: ((">MC", ">PC", ">F2b", "<SYb"),),
}
CLOSING = (
    ("<HR1a", "<HL1b", "<TR1b", "<TL1a", "<JY", "<IC", ">F1", "<AU", "<BUa", ">SYb", "<BUb"),
    (">HR1a", "<TR1a", ">HL1b", "<TL1b", ">JY", ">ZY", "<IYb", ">GYa", "<IYa", ">TR0", ">TL0", ">IC"),
    (">TR1b", ">TL1b", "<TYb", ">TR1a", ">TL1a", "<TYa", ">AU", ">IYb", ">BU"),
)
FINISH = (("image", "b", ()), ("image", "a", (">IYa",)), ("text", "b", (">TYb",)), ("text", "a", (">TYa",)))


def unit_rows(embed):
    inverse = lax.rsqrt(jnp.sum(embed * embed, axis=1, keepdims=True) + EPS)
    return embed * inverse, inverse


def kernel(
    scale_ref,
    offset_ref,
    image_ref,
    text_ref,
    image_grad_ref,
    text_grad_ref,
    imgs,
    txts,
    image_sum,
    text_sum,
    coeff_buf,
    coeff_t_buf,
    sums_out,
    sums_in,
    send_sem,
    recv_sem,
):
    rows, width = image_ref.shape
    half = rows // 2
    n_blk = lax.axis_size("blk")
    blk = lax.axis_index("blk")
    group = lax.axis_index("group")
    core = blk % 2
    y = (blk // 2) % 2

    def device(dz=0, flip=0, dx=0, flip_y=0):
        plane = (blk // 4 + dz + n_blk // 4) % (n_blk // 4)
        within = blk % 4
        if flip % 2:
            within = within + 1 - 2 * core
        if flip // 2:
            within = within + 2 - 4 * y
        x = (group % 4 + dx + 4) % 4
        upper = group // 4
        if flip_y:
            upper = 1 - upper
        return (plane * 4 + within, upper * 4 + x)

    mate, y_near, y_far = device(flip=1), device(flip=2), device(flip_y=1)
    right, left = device(dx=1), device(dx=-1)
    cross = device(dz=2 * core - 1, flip=1)
    y_on, y_back = device(dz=1 - 2 * y), device(dz=2 * y - 1)

    barrier = pltpu.get_barrier_semaphore()
    for partner in (mate, y_near, y_on, y_back, cross, right, left, y_far):
        pl.semaphore_signal(barrier, inc=1, device_id=partner, device_id_type=pl.DeviceIdType.MESH)

    def img(unit, k=0):
        return imgs, image_sum, unit, k * rows

    def txt(h, k):
        return txts, text_sum, h, k * rows

    own, own_y, on, back_, on_y, back_y = img(0), img(1), img(2 + y), img(3 - y), img(4 + y), img(5 - y)

    routes = {
        "IY": (own, own_y, y_near, y_near),
        "IC": (own, img(0, 1), mate, mate),
        "JY": (own_y, img(1, 1), mate, mate),
        "AU": (own, on, y_on, y_back),
        "BU": (own, back_, y_back, y_on),
        "GY": (own_y, on_y, y_on, y_back),
        "SY": (back_, back_y, y_near, y_near, on_y),
        "ZY": (own_y, back_y, y_back, y_on),
        "MC": (img(2), img(2, 1), mate, mate),
        "PC": (img(3), img(3, 1), mate, mate),
        "KY": (on_y, img(4 + y, 1), mate, mate),
        "LY": (back_y, img(5 - y, 1), mate, mate),
        "F1": (img(3 - core), img(6), cross, cross),
        "F2": (on_y, img(7), y_on, y_back),
        "F3": (img(7), img(7, 1), mate, mate),
        "TY": (txt(0, 0), txt(1, 0), y_far, y_far),
    }
    for h in range(2):
        routes[f"TR{h}"] = (txt(h, 0), txt(h, 3), right, left)
        routes[f"TL{h}"] = (txt(h, 0), txt(h, 1), left, right)
        routes[f"HR{h}"] = (txt(h, 3), txt(h, 2), right, left)
        routes[f"HL{h}"] = (txt(h, 1), txt(h, 2), left, right)
    names = list(routes)
    joins = {
        "F2": ("F3",),
        "GY": ("KY", "F2"),
        "SY": ("KY", "F2"),
        "ZY": ("LY",),
        "IY": ("JY", "ZY", "GY"),
        "image": ("IC", "IY", "AU", "BU"),
        "TY": ("TR1", "TL1"),
        "text": ("TR0", "TL0", "TY"),
    }
    for h in range(2):
        joins[f"TR{h}"], joins[f"TL{h}"] = (f"HR{h}",), (f"HL{h}",)
    in_place = ("MC", "PC", "F1", "SY")
    sent, added = [], set()

    def copy(index, source, target, to):
        return pltpu.make_async_remote_copy(
            src_ref=source,
            dst_ref=target,
            send_sem=send_sem.at[index],
            recv_sem=recv_sem.at[index],
            device_id=to,
            device_id_type=pl.DeviceIdType.MESH,
        )

    def at(place, part):
        return place[2], pl.ds(place[3] + part * half, half)

    def gather(name, part):
        source, target, to = routes[name][:3]
        return copy(
            2 * names.index(name) + part, source[0].at[at(source, part)], target[0].at[at(target, part)], to
        )

    def back(name, part):
        index = 2 * names.index(name) + part
        return copy(2 * len(names) + index, sums_out.at[index], sums_in.at[index], routes[name][3])

    def total(name, place, part):
        value = place[1][at(place, part)]
        for other in joins.get(name, ()):
            if (other, part) in added:
                value = value + sums_in[2 * names.index(other) + part].astype(F32)
        return value

    def act(event):
        parts = (0, 1)
        kind, name = event[0], event[1:]
        if name[-1] in "ab":
            parts, name = ("ab".index(name[-1]),), name[:-1]
        for part in parts:
            index = 2 * names.index(name) + part
            if kind == "+":
                gather(name, part).start()
                sent.append((gather, name, part))
            elif kind == "-":
                gather(name, part).wait_recv()
            elif kind == "<":
                sums_out[index] = total(name, (routes[name] + routes[name][1:2])[4], part).astype(BF16)
                back(name, part).start()
                sent.append((back, name, part))
            else:
                back(name, part).wait_recv()
                if name in in_place:
                    place = routes[name][0]
                    place[1][at(place, part)] += sums_in[index].astype(F32)
                else:
                    added.add((name, part))

    def act_all(events):
        for line in events:
            for event in line:
                act(event)

    scale = scale_ref[0]
    offset = offset_ref[0]
    unit_image, inv_image = unit_rows(image_ref[...])
    imgs[0, :rows] = unit_image.astype(BF16)
    unit_text, inv_text = unit_rows(text_ref[...])
    txts[0, :rows] = unit_text.astype(BF16)

    pl.semaphore_wait(barrier, 8)
    act_all(OPENING)
    image_sum[...] = jnp.zeros_like(image_sum)
    text_sum[...] = jnp.zeros_like(text_sum)
    imgs[6, rows:] = jnp.zeros((rows, width), BF16)

    row = lax.broadcasted_iota(jnp.int32, (rows, rows), 0)
    column = lax.broadcasted_iota(jnp.int32, (rows, rows), 1)
    diagonal = jnp.where(row == column, 1.0, 0.0).astype(F32)
    slope, level = scale * -LOG2_E, offset * -LOG2_E

    def pick(step, values):
        picked = values[0]
        for i, value in enumerate(values[1:]):
            picked = jnp.where(step > i, value, picked)
        return picked

    def tile(step, carry):
        unit = pick(step, [{8: 4 + y, 9: 5 - y}.get(u, u) for u, _ in ORDER])
        h = pick(step, [h for _, h in ORDER])
        for when, events in BEFORE.items():
            pl.when(step == when)(functools.partial(act_all, events))

        logits = lax.dot_general(
            imgs[unit], txts[h], (((1,), (1,)), ((), ())), preferred_element_type=F32
        )
        chance = 1.0 / (1.0 + jnp.exp2(logits * slope + level))
        corner = chance[:rows, :rows] - jnp.where(step == 0, 1.0, 0.0) * diagonal
        edge = jnp.concatenate([corner, chance[rows:, :rows]], axis=0)
        coeff = (scale * jnp.concatenate([edge, chance[:, rows:]], axis=1)).astype(BF16)
        coeff_buf[...] = coeff
        coeff_t_buf[...] = coeff.T
        image_sum[unit] += jnp.dot(coeff_buf[...], txts[h], preferred_element_type=F32)
        text_sum[h] += jnp.dot(coeff_t_buf[...], imgs[unit], preferred_element_type=F32)
        return carry

    lax.fori_loop(0, len(ORDER), tile, 0)
    act_all(CLOSING)

    for side, which, events in FINISH:
        act_all((events,))
        part = "ab".index(which)
        here = pl.ds(part * half, half)
        embed_ref, place, out_ref = {
            "image": (image_ref, own, image_grad_ref),
            "text": (text_ref, txt(0, 0), text_grad_ref),
        }[side]
        unit_part, inverse = unit_rows(embed_ref[here])
        direction = total(side, place, part)
        along = jnp.sum(unit_part * direction, axis=1, keepdims=True)
        out_ref[here] = (direction - unit_part * along) * inverse

    for kind, name, part in sent:
        kind(name, part).wait_send()


def per_device(picture, caption, inverse_softness, similarity_offset):
    rows, width = picture.shape
    scalar = pl.BlockSpec(memory_space=pltpu.SMEM)
    whole = pl.BlockSpec(memory_space=pltpu.VMEM)
    pairs = 15 * rows * 8 * rows
    return pl.pallas_call(
        kernel,
        out_shape=(
            jax.ShapeDtypeStruct((rows, width), F32),
            jax.ShapeDtypeStruct((rows, width), F32),
        ),
        in_specs=[scalar, scalar, whole, whole],
        out_specs=(whole, whole),
        scratch_shapes=[
            pltpu.VMEM((UNITS, 2 * rows, width), BF16),
            pltpu.VMEM((2, 4 * rows, width), BF16),
            pltpu.VMEM((UNITS, 2 * rows, width), F32),
            pltpu.VMEM((2, 4 * rows, width), F32),
            pltpu.VMEM((2 * rows, 4 * rows), BF16),
            pltpu.VMEM((4 * rows, 2 * rows), BF16),
            pltpu.VMEM((2 * MESSAGES, rows // 2, width), BF16),
            pltpu.VMEM((2 * MESSAGES, rows // 2, width), BF16),
            pltpu.SemaphoreType.DMA((4 * MESSAGES,)),
            pltpu.SemaphoreType.DMA((4 * MESSAGES,)),
        ],
        compiler_params=pltpu.CompilerParams(
            collective_id=0, has_side_effects=True, vmem_limit_bytes=56 * 2**20
        ),
        cost_estimate=pl.CostEstimate(
            flops=6 * pairs * width, bytes_accessed=16 * rows * width, transcendentals=2 * pairs
        ),
    )(inverse_softness, similarity_offset, picture, caption)


def solution(mesh):
    spec = P(("blk", "group"), None)
    return jax.shard_map(
        per_device,
        mesh=mesh,
        in_specs=(spec, spec, P(), P()),
        out_specs=(spec, spec),
        check_vma=False,
    )
```

time: 89.2 us -> 81.9 us (0.918)
  Pallas kernels: 83.4 us -> 76.4 us
    pallas_call x1, Pallas kernels: 83.4 us -> 76.4 us  [per_device(): pl.pallas_call(kernel, out_shape=(jax.ShapeDtypeStruct((rows, width), F32...]
where the time goes in v3:
time: 81.9 us; the launch traced here: 81.1 us
  Pallas kernels  76.4 us (93%)
  local copies, waits for them, and re-layouts  2.8 us (3%)
  between operations  1.94 us (2%)
    pallas_call x1, Pallas kernels, per_device(): pl.pallas_call(kernel, out_shape=(jax.ShapeDtypeStruct((rows, width), F32...  76.4 us
    unnamed x4, local copies, waits for them, and re-layouts  2.8 us

profile of v3, /device:TPU:1, one launch (start us, length us, event | category | flops | bytes accessed | tf_op | source)
XLA Modules:
  0.0 81.1 jit_solution(16144805635243626616)
XLA Ops:
  1.9 76.4 %shard_map.59 = (f32[128,1152]{1,0:T(8,128)}, f32[128,1152]{1,0:T(8,128)}) custom-call(f32[1]{0:T(128)S(6)} %copy.8.scale_ref, f32[1]{0:T(128)S(6)} %copy.9.offset_ref, f32[128,1152]{1,0:T(8,128)} %image_ref.1, f32[128,1152]{1,0:T(8,128)} %text_ref.1), custom_call_target="tpu_custom_call" | custom-call | flops 13589544960 | bytes 2359296 | tf_op jit(solution)/shard_map/pallas_call | solution.py:282
  78.3 0.0 copy-start
  78.3 2.0 %copy.10 = f32[128,1152]{1,0:T(8,128)} copy(f32[128,1152]{1,0:T(8,128)} %get-tuple-element.4) | data formatting | bytes 1179648
  80.3 0.0 copy-done
  80.3 0.8 %copy.11 = f32[128,1152]{1,0:T(8,128)} copy(f32[128,1152]{1,0:T(8,128)S(1)} %copy-done) | data formatting | bytes 1179648
Async XLA Ops:
  78.3 2.0 %copy-start = (f32[128,1152]{1,0:T(8,128)S(1)}, f32[128,1152]{1,0:T(8,128)}, u32[]{:S(2)}) copy-start(f32[128,1152]{1,0:T(8,128)} %get-tuple-element.5) | copy-start | bytes 1769476

commit v4 on v3

--- a/solution.py
+++ b/solution.py
@@ -16,40 +16,45 @@
 MESSAGES = 24
 
 OPENING = (
-    ("+IYa", "+TYa", "+AUa", "+BUa", "+TR0a", "+TL0b", "+TYb", "+AUb", "+BUb", "+TR0b", "+TL0a", "+IC"),
+    ("+TYa", "+IYa", "+AUa", "+BUa", "+TR0a", "+TL0b", "+TYb", "+IYb", "+AUb", "+BUb", "+TR0b", "+TL0a", "+IC"),
 )
 ORDER = (
-    (0, 0), (2, 0), (3, 0), (6, 0), (1, 0), (8, 0), (7, 0), (9, 0),
-    (7, 1), (6, 1), (8, 1), (9, 1), (2, 1), (3, 1), (1, 1), (0, 1),
+    (0, 0), (2, 0), (3, 0), (1, 0), (6, 0), (8, 0), (1, 1), (6, 1),
+    (9, 0), (7, 0), (7, 1), (9, 1), (8, 1), (2, 1), (3, 1), (0, 1),
 )
 BEFORE = {
     0: (
-        ("-IYa", "+GYa", "+ZYa", "+JYa", "-AUa", "-BUa", "+MCa", "+PCa", "-TR0a", "+HR0a", "-TL0b", "+HL0b"),
-        ("-TYa", "+TR1a", "+TL1a", "-AUb", "-BUb", "+SYb", "+IYb", "+F1", "+MCb", "+PCb"),
+        ("-TR0a", "+HR0a", "-TL0b", "+HL0b", "-TYa", "+TR1a", "+TL1a", "-AUa", "-BUa", "+MCa", "+PCa"),
+        ("-IYa", "+GYa", "+ZYa", "+JYa", "-AUb", "-BUb", "+SYb", "+F1", "+MCb", "+PCb"),
         ("-TYb", "+TR1b", "+TL1b", "-IC", "-TR0b", "-TL0a", "-HR0a", "-HL0b"),
     ),
     1: (("-GYa", "+F2a", "+KYa", "-MC", "-PC"),),
-    2: (("-TR1a", "+HR1a", "-TL1b", "+HL1b"),),
-    3: (("-SYb", "+F2b", "+KYb", "-F1"),),
-    4: (("-IYb", "+ZYb", "+JYb", "-JY"),),
-    5: (("-ZYa", "+LYa", "-KY"),),
-    6: (("-F2a", "+F3a", "-F2b", "+F3b", "-F3"),),
-    7: (("-ZYb", "+LYb", "-LY"),),
-    8: (("<HR0a", "<HL0b", "<TR0b", "<TL0a", "-TR1b", "-TL1a", "-HR1a", "-HL1b"),),
-    9: (("<F3",),),
-    10: ((">F3a", "<F2a", ">F3b", "<F2b", "<F1"),),
-    11: (("<KY",),),
-    12: (("<LY", ">KY", ">HR0a", "<TR0a", ">HL0b", "<TL0b"),),
-    13: ((">LY", "<ZY"),),
-    14: (("<MC", "<PC", ">F2a", "<GYa"),),
-    15: ((">MC", ">PC", ">F2b", "<SYb"),),
+    2: (("-IYb", "+ZYb", "+JYb"),),
+    3: (("-JY", "-TR1a", "+HR1a", "-TL1b", "+HL1b"),),
+    4: (("-F1", "-SYb", "+F2b", "+KYb"),),
+    5: (("-KY", "-ZYa", "+LYa"),),
+    6: (("-ZYb", "+LYb", "-TR1b", "-TL1a", "-HR1a", "-HL1b"),),
+    7: (("-F2a", "+F3a", "<JY"),),
+    8: (("-LY", "-F2b", "+F3b", "<F1"),),
+    9: (("-F3",),),
+    10: (("<HR0a", "<HL0b", "<TR0b", "<TL0a"),),
+    11: (("<F3",),),
+    12: (("<LY", ">F3a", "<F2a", ">F3b", "<F2b"),),
+    13: ((">LY", "<ZY", "<KY"),),
+    14: ((">HR0a", "<TR0a", ">HL0b", "<TL0b", ">KY", ">F1", ">JY"),),
+    15: (("<MC", "<PC"),),
 }
 CLOSING = (
-    ("<HR1a", "<HL1b", "<TR1b", "<TL1a", "<JY", "<IC", ">F1", "<AU", "<BUa", ">SYb", "<BUb"),
-    (">HR1a", "<TR1a", ">HL1b", "<TL1b", ">JY", ">ZY", "<IYb", ">GYa", "<IYa", ">TR0", ">TL0", ">IC"),
-    (">TR1b", ">TL1b", "<TYb", ">TR1a", ">TL1a", "<TYa", ">AU", ">IYb", ">BU"),
+    ("<HR1a", "<HL1b", "<TR1b", "<TL1a", ">F2a", "<GYa", "<IC", ">MC", ">PC", "<AU", "<BUa", ">F2b", "<SYb"),
+    (">ZYb", "<IYb", ">HR1a", "<TR1a", ">HL1b", "<TL1b", ">ZYa", ">GYa", "<IYa", ">SYb", "<BUb"),
+    (">TR1b", ">TL1b", "<TYb", ">TR1a", ">TL1a", "<TYa", ">TR0", ">TL0", ">IC", ">AU", ">BUa"),
 )
-FINISH = (("image", "b", ()), ("image", "a", (">IYa",)), ("text", "b", (">TYb",)), ("text", "a", (">TYa",)))
+FINISH = (
+    ("image", "a", (">IYa",)),
+    ("image", "b", (">IYb", ">BUb")),
+    ("text", "b", (">TYb",)),
+    ("text", "a", (">TYa",)),
+)
 
 
 def unit_rows(embed):

time: 81.9 us -> 77.6 us (0.947)
  Pallas kernels: 76.4 us -> 72.8 us
    pallas_call x1, Pallas kernels: 76.4 us -> 72.8 us  [per_device(): pl.pallas_call(kernel, out_shape=(jax.ShapeDtypeStruct((rows, width), F32...]
where the time goes in v4:
time: 77.6 us; the launch traced here: 77.5 us
  Pallas kernels  72.8 us (94%)
  local copies, waits for them, and re-layouts  2.8 us (4%)
  between operations  1.94 us (2%)
    pallas_call x1, Pallas kernels, per_device(): pl.pallas_call(kernel, out_shape=(jax.ShapeDtypeStruct((rows, width), F32...  72.8 us
    unnamed x4, local copies, waits for them, and re-layouts  2.8 us

profile of v4, /device:TPU:1, one launch (start us, length us, event | category | flops | bytes accessed | tf_op | source)
XLA Modules:
  0.0 77.5 jit_solution(4130934494561011184)
XLA Ops:
  1.9 72.8 %shard_map.59 = (f32[128,1152]{1,0:T(8,128)}, f32[128,1152]{1,0:T(8,128)}) custom-call(f32[1]{0:T(128)S(6)} %copy.8.scale_ref, f32[1]{0:T(128)S(6)} %copy.9.offset_ref, f32[128,1152]{1,0:T(8,128)} %image_ref.1, f32[128,1152]{1,0:T(8,128)} %text_ref.1), custom_call_target="tpu_custom_call" | custom-call | flops 13589544960 | bytes 2359296 | tf_op jit(solution)/shard_map/pallas_call | solution.py:287
  74.7 0.0 copy-start
  74.7 2.0 %copy.10 = f32[128,1152]{1,0:T(8,128)} copy(f32[128,1152]{1,0:T(8,128)} %get-tuple-element.4) | data formatting | bytes 1179648
  76.7 0.0 copy-done
  76.7 0.8 %copy.11 = f32[128,1152]{1,0:T(8,128)} copy(f32[128,1152]{1,0:T(8,128)S(1)} %copy-done) | data formatting | bytes 1179648
Async XLA Ops:
  74.7 2.0 %copy-start = (f32[128,1152]{1,0:T(8,128)S(1)}, f32[128,1152]{1,0:T(8,128)}, u32[]{:S(2)}) copy-start(f32[128,1152]{1,0:T(8,128)} %get-tuple-element.5) | copy-start | bytes 1769476

commit v5 on v4

--- a/solution.py
+++ b/solution.py
@@ -16,7 +16,8 @@
 MESSAGES = 24
 
 OPENING = (
-    ("+TYa", "+IYa", "+AUa", "+BUa", "+TR0a", "+TL0b", "+TYb", "+IYb", "+AUb", "+BUb", "+TR0b", "+TL0a", "+IC"),
+    ("+TYa", "+IYa", "+AUa", "+BUa", "+TR0a", "+TL0b", "+TYb", "+AUb", "+BUb", "+TR0b",),
+    ("+TL0a", "+IC",),
 )
 ORDER = (
     (0, 0), (2, 0), (3, 0), (1, 0), (6, 0), (8, 0), (1, 1), (6, 1),
@@ -24,30 +25,61 @@
 )
 BEFORE = {
     0: (
-        ("-TR0a", "+HR0a", "-TL0b", "+HL0b", "-TYa", "+TR1a", "+TL1a", "-AUa", "-BUa", "+MCa", "+PCa"),
-        ("-IYa", "+GYa", "+ZYa", "+JYa", "-AUb", "-BUb", "+SYb", "+F1", "+MCb", "+PCb"),
-        ("-TYb", "+TR1b", "+TL1b", "-IC", "-TR0b", "-TL0a", "-HR0a", "-HL0b"),
-    ),
-    1: (("-GYa", "+F2a", "+KYa", "-MC", "-PC"),),
-    2: (("-IYb", "+ZYb", "+JYb"),),
-    3: (("-JY", "-TR1a", "+HR1a", "-TL1b", "+HL1b"),),
-    4: (("-F1", "-SYb", "+F2b", "+KYb"),),
-    5: (("-KY", "-ZYa", "+LYa"),),
-    6: (("-ZYb", "+LYb", "-TR1b", "-TL1a", "-HR1a", "-HL1b"),),
-    7: (("-F2a", "+F3a", "<JY"),),
-    8: (("-LY", "-F2b", "+F3b", "<F1"),),
-    9: (("-F3",),),
-    10: (("<HR0a", "<HL0b", "<TR0b", "<TL0a"),),
-    11: (("<F3",),),
-    12: (("<LY", ">F3a", "<F2a", ">F3b", "<F2b"),),
-    13: ((">LY", "<ZY", "<KY"),),
-    14: ((">HR0a", "<TR0a", ">HL0b", "<TL0b", ">KY", ">F1", ">JY"),),
-    15: (("<MC", "<PC"),),
+        ("-TR0a", "+HR0a", "-TL0b", "+HL0b", "-TYa", "+TR1a", "+TL1a", "-AUa", "-BUa", "+MCa",),
+        ("+PCa", "-IYa", "+GYa", "+ZYa", "+JYa", "-AUb", "-BUb", "+SYb", "+IYb", "+F1",),
+        ("+MCb", "+PCb", "-TYb", "+TR1b", "+TL1b", "-IC", "-TR0b", "-TL0a", "-HR0a", "-HL0b",),
+    ),
+    1: (
+        ("-GYa", "+F2a", "+KYa", "-MC", "-PC",),
+    ),
+    2: (
+        ("-IYb", "+ZYb", "+JYb",),
+    ),
+    3: (
+        ("-JY", "-TR1a", "+HR1a", "-TL1b", "+HL1b",),
+    ),
+    4: (
+        ("-F1", "-SYb", "+F2b", "+KYb",),
+    ),
+    5: (
+        ("-KY", "-ZYa", "+LYa",),
+    ),
+    6: (
+        ("-ZYb", "+LYb", "-TR1b", "-TL1a", "-HR1a", "-HL1b",),
+    ),
+    7: (
+        ("-F2a", "+F3a", "<JY",),
+    ),
+    8: (
+        ("-LY", "-F2b", "+F3b", "<F1",),
+    ),
+    9: (
+        ("-F3",),
+    ),
+    10: (
+        ("<HR0a", "<HL0b", "<TR0b", "<TL0a",),
+    ),
+    11: (
+        ("<F3",),
+    ),
+    12: (
+        ("<LY", ">F3a", "<F2a", ">F3b", "<F2b",),
+    ),
+    13: (
+        (">LY", "<ZY", "<KY",),
+    ),
+    14: (
+        (">HR0a", "<TR0a", ">HL0b", "<TL0b", ">KY", ">F1", ">JY",),
+    ),
+    15: (
+        ("<MC", "<PC",),
+    ),
 }
 CLOSING = (
-    ("<HR1a", "<HL1b", "<TR1b", "<TL1a", ">F2a", "<GYa", "<IC", ">MC", ">PC", "<AU", "<BUa", ">F2b", "<SYb"),
-    (">ZYb", "<IYb", ">HR1a", "<TR1a", ">HL1b", "<TL1b", ">ZYa", ">GYa", "<IYa", ">SYb", "<BUb"),
-    (">TR1b", ">TL1b", "<TYb", ">TR1a", ">TL1a", "<TYa", ">TR0", ">TL0", ">IC", ">AU", ">BUa"),
+    ("<HR1a", "<HL1b", "<TR1b", "<TL1a", ">F2a", "<GYa", "<IC", ">MC", ">PC", "<AU",),
+    ("<BUa", ">F2b", "<SYb", ">ZYb", "<IYb", ">HR1a", "<TR1a", ">HL1b", "<TL1b", ">ZYa",),
+    (">GYa", "<IYa", ">SYb", "<BUb", ">TR1b", ">TL1b", "<TYb", ">TR1a", ">TL1a", "<TYa",),
+    (">TR0", ">TL0", ">IC", ">AU", ">BUa",),
 )
 FINISH = (
     ("image", "a", (">IYa",)),
@@ -67,8 +99,7 @@
     offset_ref,
     image_ref,
     text_ref,
-    image_grad_ref,
-    text_grad_ref,
+    grads_ref,
     imgs,
     txts,
     image_sum,
@@ -267,8 +298,8 @@
         part = "ab".index(which)
         here = pl.ds(part * half, half)
         embed_ref, place, out_ref = {
-            "image": (image_ref, own, image_grad_ref),
-            "text": (text_ref, txt(0, 0), text_grad_ref),
+            "image": (image_ref, own, grads_ref.at[0]),
+            "text": (text_ref, txt(0, 0), grads_ref.at[1]),
         }[side]
         unit_part, inverse = unit_rows(embed_ref[here])
         direction = total(side, place, part)
@@ -284,14 +315,11 @@
     scalar = pl.BlockSpec(memory_space=pltpu.SMEM)
     whole = pl.BlockSpec(memory_space=pltpu.VMEM)
     pairs = 15 * rows * 8 * rows
-    return pl.pallas_call(
+    grads = pl.pallas_call(
         kernel,
-        out_shape=(
-            jax.ShapeDtypeStruct((rows, width), F32),
-            jax.ShapeDtypeStruct((rows, width), F32),
-        ),
+        out_shape=jax.ShapeDtypeStruct((2, rows, width), F32),
         in_specs=[scalar, scalar, whole, whole],
-        out_specs=(whole, whole),
+        out_specs=whole,
         scratch_shapes=[
             pltpu.VMEM((UNITS, 2 * rows, width), BF16),
             pltpu.VMEM((2, 4 * rows, width), BF16),
@@ -311,6 +339,7 @@
             flops=6 * pairs * width, bytes_accessed=16 * rows * width, transcendentals=2 * pairs
         ),
     )(inverse_softness, similarity_offset, picture, caption)
+    return grads[0], grads[1]
 
 
 def solution(mesh):

time: 77.6 us -> 76.8 us (0.990); the launches traced: 77.5 us -> 75.9 us
  Pallas kernels: 72.8 us -> 71.6 us
    unnamed x4 -> x0, local copies, waits for them, and re-layouts: 2.8 us -> none
    squeeze x0 -> x1, local copies, waits for them, and re-layouts: none -> 2.33 us  [per_device(): return (grads[0], grads[1])]
    pallas_call x1, Pallas kernels: 72.8 us -> 71.6 us  [per_device(): pl.pallas_call(kernel, out_shape=jax.ShapeDtypeStruct((2, rows, width), F...]
where the time goes in v5:
time: 76.8 us; the launch traced here: 75.9 us
  Pallas kernels  71.6 us (93%)
  local copies, waits for them, and re-layouts  2.33 us (3%)
  between operations  1.93 us (3%)
    pallas_call x1, Pallas kernels, per_device(): pl.pallas_call(kernel, out_shape=jax.ShapeDtypeStruct((2, rows, width), F...  71.6 us
    squeeze x1, local copies, waits for them, and re-layouts, per_device(): return (grads[0], grads[1])  2.33 us

profile of v5, /device:TPU:1, one launch (start us, length us, event | category | flops | bytes accessed | tf_op | source)
XLA Modules:
  0.0 75.9 jit_solution(6413566913645635009)
XLA Ops:
  1.9 71.6 %shard_map.59 = f32[2,128,1152]{2,1,0:T(8,128)} custom-call(f32[1]{0:T(128)S(6)} %copy.6.scale_ref, f32[1]{0:T(128)S(6)} %copy.7.offset_ref, f32[128,1152]{1,0:T(8,128)} %image_ref.1, f32[128,1152]{1,0:T(8,128)} %text_ref.1), custom_call_target="tpu_custom_call" | custom-call | flops 13589544960 | bytes 2359296 | tf_op jit(solution)/shard_map/pallas_call | solution.py:318
  73.6 2.3 %slice_bitcast_fusion = (f32[128,1152]{1,0:T(8,128)}, f32[128,1152]{1,0:T(8,128)}) fusion(f32[2,128,1152]{2,1,0:T(8,128)} %shard_map.59), kind=kLoop, calls=%fused_computation | loop fusion | bytes 2359296 | tf_op jit(solution)/shard_map/squeeze | solution.py:342

commit v6 on v5

--- a/solution.py
+++ b/solution.py
@@ -108,8 +108,10 @@
     coeff_t_buf,
     sums_out,
     sums_in,
+    grads,
     send_sem,
     recv_sem,
+    out_sem,
 ):
     rows, width = image_ref.shape
     half = rows // 2
@@ -293,21 +295,29 @@
     lax.fori_loop(0, len(ORDER), tile, 0)
     act_all(CLOSING)
 
+    written = []
     for side, which, events in FINISH:
-        act_all((events,))
         part = "ab".index(which)
         here = pl.ds(part * half, half)
-        embed_ref, place, out_ref = {
-            "image": (image_ref, own, grads_ref.at[0]),
-            "text": (text_ref, txt(0, 0), grads_ref.at[1]),
+        embed_ref, place, out = {
+            "image": (image_ref, own, 0),
+            "text": (text_ref, txt(0, 0), 1),
         }[side]
         unit_part, inverse = unit_rows(embed_ref[here])
+        act_all((events,))
         direction = total(side, place, part)
         along = jnp.sum(unit_part * direction, axis=1, keepdims=True)
-        out_ref[here] = (direction - unit_part * along) * inverse
+        grads[out, here] = (direction - unit_part * along) * inverse
+        write = pltpu.make_async_copy(
+            grads.at[out, here], grads_ref.at[out, here], out_sem.at[len(written)]
+        )
+        write.start()
+        written.append(write)
 
     for kind, name, part in sent:
         kind(name, part).wait_send()
+    for write in written:
+        write.wait()
 
 
 def per_device(picture, caption, inverse_softness, similarity_offset):
@@ -319,7 +329,7 @@
         kernel,
         out_shape=jax.ShapeDtypeStruct((2, rows, width), F32),
         in_specs=[scalar, scalar, whole, whole],
-        out_specs=whole,
+        out_specs=pl.BlockSpec(memory_space=pl.ANY),
         scratch_shapes=[
             pltpu.VMEM((UNITS, 2 * rows, width), BF16),
             pltpu.VMEM((2, 4 * rows, width), BF16),
@@ -329,8 +339,10 @@
             pltpu.VMEM((4 * rows, 2 * rows), BF16),
             pltpu.VMEM((2 * MESSAGES, rows // 2, width), BF16),
             pltpu.VMEM((2 * MESSAGES, rows // 2, width), BF16),
+            pltpu.VMEM((2, rows, width), F32),
             pltpu.SemaphoreType.DMA((4 * MESSAGES,)),
             pltpu.SemaphoreType.DMA((4 * MESSAGES,)),
+            pltpu.SemaphoreType.DMA((len(FINISH),)),
         ],
         compiler_params=pltpu.CompilerParams(
             collective_id=0, has_side_effects=True, vmem_limit_bytes=56 * 2**20

time: 76.8 us -> 76.3 us (level)
  no operation moved by 1% of the time
where the time goes in v6:
time: 76.3 us; the launch traced here: 75.5 us
  Pallas kernels  71.2 us (93%)
  local copies, waits for them, and re-layouts  2.33 us (3%)
  between operations  1.93 us (3%)
    pallas_call x1, Pallas kernels, per_device(): pl.pallas_call(kernel, out_shape=jax.ShapeDtypeStruct((2, rows, width), F...  71.2 us
    squeeze x1, local copies, waits for them, and re-layouts, per_device(): return (grads[0], grads[1])  2.33 us

profile of v6, /device:TPU:1, one launch (start us, length us, event | category | flops | bytes accessed | tf_op | source)
XLA Modules:
  0.0 75.5 jit_solution(10441035144264632142)
XLA Ops:
  1.9 71.2 %shard_map.59 = f32[2,128,1152]{2,1,0:T(8,128)} custom-call(f32[1]{0:T(128)S(6)} %copy.6.scale_ref, f32[1]{0:T(128)S(6)} %copy.7.offset_ref, f32[128,1152]{1,0:T(8,128)} %image_ref.1, f32[128,1152]{1,0:T(8,128)} %text_ref.1), custom_call_target="tpu_custom_call" | custom-call | flops 13589544960 | bytes 2359296 | tf_op jit(solution)/shard_map/pallas_call | solution.py:328
  73.1 2.3 %slice_bitcast_fusion = (f32[128,1152]{1,0:T(8,128)}, f32[128,1152]{1,0:T(8,128)}) fusion(f32[2,128,1152]{2,1,0:T(8,128)} %shard_map.59), kind=kLoop, calls=%fused_computation | loop fusion | bytes 2359296 | tf_op jit(solution)/shard_map/squeeze | solution.py:354

commit v7 on v6

--- a/solution.py
+++ b/solution.py
@@ -16,8 +16,8 @@
 MESSAGES = 24
 
 OPENING = (
-    ("+TYa", "+IYa", "+AUa", "+BUa", "+TR0a", "+TL0b", "+TYb", "+AUb", "+BUb", "+TR0b",),
-    ("+TL0a", "+IC",),
+    ("+TYa", "+TR0a", "+TL0b", "+TYb", "+TR0b", "+TL0a"),
+    ("+IYa", "+AUa", "+BUa", "+AUb", "+BUb", "+IC"),
 )
 ORDER = (
     (0, 0), (2, 0), (3, 0), (1, 0), (6, 0), (8, 0), (1, 1), (6, 1),
@@ -251,13 +251,12 @@
 
     scale = scale_ref[0]
     offset = offset_ref[0]
-    unit_image, inv_image = unit_rows(image_ref[...])
-    imgs[0, :rows] = unit_image.astype(BF16)
-    unit_text, inv_text = unit_rows(text_ref[...])
-    txts[0, :rows] = unit_text.astype(BF16)
+    txts[0, :rows] = unit_rows(text_ref[...])[0].astype(BF16)
 
     pl.semaphore_wait(barrier, 8)
-    act_all(OPENING)
+    act_all(OPENING[:1])
+    imgs[0, :rows] = unit_rows(image_ref[...])[0].astype(BF16)
+    act_all(OPENING[1:])
     image_sum[...] = jnp.zeros_like(image_sum)
     text_sum[...] = jnp.zeros_like(text_sum)
     imgs[6, rows:] = jnp.zeros((rows, width), BF16)

time: 76.3 us -> 78.7 us (1.031)
  Pallas kernels: 71.2 us -> 74.3 us
    pallas_call x1, Pallas kernels: 71.2 us -> 74.3 us  [per_device(): pl.pallas_call(kernel, out_shape=jax.ShapeDtypeStruct((2, rows, width), F...]
where the time goes in v7:
time: 78.7 us; the launch traced here: 78.6 us
  Pallas kernels  74.3 us (94%)
  local copies, waits for them, and re-layouts  2.33 us (3%)
  between operations  1.93 us (2%)
    pallas_call x1, Pallas kernels, per_device(): pl.pallas_call(kernel, out_shape=jax.ShapeDtypeStruct((2, rows, width), F...  74.3 us
    squeeze x1, local copies, waits for them, and re-layouts, per_device(): return (grads[0], grads[1])  2.33 us

profile of v7, /device:TPU:1, one launch (start us, length us, event | category | flops | bytes accessed | tf_op | source)
XLA Modules:
  0.0 78.6 jit_solution(17737695627492179504)
XLA Ops:
  1.9 74.3 %shard_map.59 = f32[2,128,1152]{2,1,0:T(8,128)} custom-call(f32[1]{0:T(128)S(6)} %copy.6.scale_ref, f32[1]{0:T(128)S(6)} %copy.7.offset_ref, f32[128,1152]{1,0:T(8,128)} %image_ref.1, f32[128,1152]{1,0:T(8,128)} %text_ref.1), custom_call_target="tpu_custom_call" | custom-call | flops 13589544960 | bytes 2359296 | tf_op jit(solution)/shard_map/pallas_call | solution.py:327
  76.3 2.3 %slice_bitcast_fusion = (f32[128,1152]{1,0:T(8,128)}, f32[128,1152]{1,0:T(8,128)}) fusion(f32[2,128,1152]{2,1,0:T(8,128)} %shard_map.59), kind=kLoop, calls=%fused_computation | loop fusion | bytes 2359296 | tf_op jit(solution)/shard_map/squeeze | solution.py:353

commit v8 on v6

--- a/solution.py
+++ b/solution.py
@@ -16,7 +16,7 @@
 MESSAGES = 24
 
 OPENING = (
-    ("+TYa", "+IYa", "+AUa", "+BUa", "+TR0a", "+TL0b", "+TYb", "+AUb", "+BUb", "+TR0b",),
+    ("+IYa", "+AUa", "+BUa", "+TYa", "+TR0a", "+TL0b", "+TYb", "+AUb", "+BUb", "+TR0b",),
     ("+TL0a", "+IC",),
 )
 ORDER = (

time: 76.3 us -> 76.4 us (level)
  no operation moved by 1% of the time
where the time goes in v8:
time: 76.4 us; the launch traced here: 75.2 us
  Pallas kernels  70.9 us (93%)
  local copies, waits for them, and re-layouts  2.33 us (3%)
  between operations  1.93 us (3%)
    pallas_call x1, Pallas kernels, per_device(): pl.pallas_call(kernel, out_shape=jax.ShapeDtypeStruct((2, rows, width), F...  70.9 us
    squeeze x1, local copies, waits for them, and re-layouts, per_device(): return (grads[0], grads[1])  2.33 us

profile of v8, /device:TPU:1, one launch (start us, length us, event | category | flops | bytes accessed | tf_op | source)
XLA Modules:
  0.0 75.2 jit_solution(7019562438301087712)
XLA Ops:
  1.9 70.9 %shard_map.59 = f32[2,128,1152]{2,1,0:T(8,128)} custom-call(f32[1]{0:T(128)S(6)} %copy.6.scale_ref, f32[1]{0:T(128)S(6)} %copy.7.offset_ref, f32[128,1152]{1,0:T(8,128)} %image_ref.1, f32[128,1152]{1,0:T(8,128)} %text_ref.1), custom_call_target="tpu_custom_call" | custom-call | flops 13589544960 | bytes 2359296 | tf_op jit(solution)/shard_map/pallas_call | solution.py:328
  72.8 2.3 %slice_bitcast_fusion = (f32[128,1152]{1,0:T(8,128)}, f32[128,1152]{1,0:T(8,128)}) fusion(f32[2,128,1152]{2,1,0:T(8,128)} %shard_map.59), kind=kLoop, calls=%fused_computation | loop fusion | bytes 2359296 | tf_op jit(solution)/shard_map/squeeze | solution.py:354
